TPU v7x, 32 devices: a whole 2x2x4 slice. The times are simulated.
32 devices in a mesh: nodes: 8 (over z, y), rep: 4 (over x, core).
Axes of the slice: x: 2, y: 2, z: 4, core: 2. Of those that a mesh axis runs over, the one named last changes fastest.
Arguments:
- memory: float32 [4096, 512], P('nodes'), may hold values from -16 to 16
- last_tick: int32 [4096], P('nodes'), may hold values from 0 to 499
- src_local: int32 [4096], P(('nodes', 'rep')), may hold values from 0 to 511
- dst_owner: int32 [4096, 1], P(('nodes', 'rep')), may hold values from 0 to 7; in each aligned block of 128 rows (0 to 127, 128 to 255, ...) at most 32 rows name the same one
- dst_local: int32 [4096], P(('nodes', 'rep')), may hold values from 0 to 511
- event_tick: int32 [4096], P(('nodes', 'rep')), may hold values from 500 to 999
- nbr_owner: int32 [4096, 16, 1], P(('nodes', 'rep')), may hold values from 0 to 7; in each aligned block of 2048 rows (0 to 2047, 2048 to 4095, ..., all dimensions but the last counted through in order) at most 512 rows name the same one
- nbr_local: int32 [4096, 16], P(('nodes', 'rep')), may hold values from 0 to 511
- nbr_tick: int32 [4096, 16], P(('nodes', 'rep')), may hold values from 0 to 499
- freq: float32 [128], replicated, may hold values from 0.002 to 0.5
- phase: float32 [128], replicated, may hold values from -3.140625 to 3.140625
- w_message: bfloat16 [1152, 512], replicated, may hold values from -0.1875 to 0.1875
- gru_input: float32 [3, 512, 512], P(None, None, 'rep'), may hold values from -0.5 to 0.5
- gru_hidden: float32 [3, 512, 512], P(None, None, 'rep'), may hold values from -0.25 to 0.25
- gru_bias: float32 [4, 512], P(None, 'rep'), may hold values from -3 to 3
- w_query: bfloat16 [512, 512], replicated, may hold values from -1 to 1
- w_keyval_mem: bfloat16 [512, 1024], replicated, may hold values from -0.25 to 0.25
- w_keyval_time: bfloat16 [128, 1024], replicated, may hold values from -0.5 to 0.5
Outputs:
- new_memory: float32 [4096, 512], P('nodes', 'rep')
- embed: bfloat16 [4096, 512], P(('nodes', 'rep'))
Inputs may be any that keep to these rules, and one draw needn't show every extreme that they name: `dst_owner`: on one device no owner is named by more than 32 events. `nbr_owner`: on one device no owner is named by more than 512 neighbour entries.
All inputs are finite; a program needn't handle non-finite values.
Results may differ from a plain program's by a relative error of at most 0.012.
The roundings to bfloat16 on the way count: a program that leaves them out, or rounds other values in their place, can miss the bound.
Values may be sent and summed in bfloat16 or wider, within the bound.
A program may use at most 128 MiB of HBM per device.

v0:
```python
import math

import jax
import jax.numpy as jnp
from jax import lax
from jax.sharding import PartitionSpec as P

HEADS = 8
HEAD_DIM = 64


def encode(gaps, freq, phase):
    return jnp.cos(gaps[..., None] * freq + phase)


def place(owner, groups, capacity):
    onehot = (owner[:, None] == jnp.arange(groups, dtype=jnp.int32)[None, :]).astype(jnp.int32)
    before = jnp.cumsum(onehot, axis=0) - onehot
    return owner * capacity + jnp.sum(before * onehot, axis=1)


def message_pair(src_rows, dst_rows, src_time, dst_time, w_message):
    count = src_rows.shape[0]
    stacked = jnp.concatenate(
        [
            jnp.concatenate([src_rows, dst_rows, src_time], axis=1),
            jnp.concatenate([dst_rows, src_rows, dst_time], axis=1),
        ],
        axis=0,
    )
    messages = jax.nn.silu(jnp.dot(stacked, w_message, preferred_element_type=jnp.float32)).astype(
        jnp.bfloat16
    )
    return (messages[:count], messages[count:])


def on_device(
    memory,
    last_tick,
    src_local,
    dst_owner,
    dst_local,
    event_tick,
    nbr_owner,
    nbr_local,
    nbr_tick,
    freq,
    phase,
    w_message,
    gru_input,
    gru_hidden,
    gru_bias,
    w_query,
    w_keyval_mem,
    w_keyval_time,
):
    groups = lax.axis_size("nodes")
    events = src_local.shape[0]
    rows_here = memory.shape[0]
    width_m = memory.shape[1]
    neighbours = nbr_local.shape[1]
    msg_width = w_message.shape[1]
    dst_cap = max(2, 2 * events // groups)
    nbr_cap = 2 * events * neighbours // groups
    dst_slot = place(dst_owner[:, 0], groups, dst_cap)
    nbr_slot = place(nbr_owner.reshape(-1), groups, nbr_cap)
    dst_ids = (
        jnp.full((groups * dst_cap,), -1, jnp.int32)
        .at[dst_slot]
        .set(dst_local)
        .reshape(groups, dst_cap)
    )
    nbr_ids = (
        jnp.full((groups * nbr_cap,), -1, jnp.int32)
        .at[nbr_slot]
        .set(nbr_local.reshape(-1))
        .reshape(groups, nbr_cap)
    )
    mem_half = memory.astype(jnp.bfloat16)
    near_rows = mem_half[src_local]
    near_ticks = last_tick[src_local]
    ticks = event_tick.astype(jnp.float32)
    got_dst, got_nbr = (
        lax.all_to_all(dst_ids, "nodes", split_axis=0, concat_axis=0, tiled=True),
        lax.all_to_all(nbr_ids, "nodes", split_axis=0, concat_axis=0, tiled=True),
    )
    safe_dst = jnp.maximum(got_dst, 0)
    reply_rows, reply_ticks = (
        lax.all_to_all(mem_half[safe_dst], "nodes", split_axis=0, concat_axis=0, tiled=True),
        lax.all_to_all(last_tick[safe_dst], "nodes", split_axis=0, concat_axis=0, tiled=True),
    )
    far_rows = reply_rows.reshape(-1, width_m)[dst_slot]
    far_ticks = reply_ticks.reshape(-1)[dst_slot]
    src_time = encode(ticks - near_ticks.astype(jnp.float32), freq, phase).astype(jnp.bfloat16)
    dst_time = encode(ticks - far_ticks.astype(jnp.float32), freq, phase).astype(jnp.bfloat16)
    msg_src, msg_dst = message_pair(near_rows, far_rows, src_time, dst_time, w_message)
    outgoing = (
        jnp.zeros((groups * dst_cap, msg_width), jnp.bfloat16)
        .at[dst_slot]
        .set(msg_dst)
        .reshape(groups, dst_cap, msg_width)
    )
    incoming = lax.all_to_all(outgoing, "nodes", split_axis=0, concat_axis=0, tiled=True)
    far_msgs = incoming.reshape(-1, msg_width)
    row_ids = jnp.arange(rows_here, dtype=jnp.int32)[:, None]
    hit_far = (row_ids == got_dst.reshape(1, -1)).astype(jnp.bfloat16)
    hit_near = (row_ids == src_local[None, :]).astype(jnp.bfloat16)
    sums = jnp.dot(hit_near, msg_src, preferred_element_type=jnp.float32) + jnp.dot(
        hit_far, far_msgs, preferred_element_type=jnp.float32
    )
    counts = jnp.sum(hit_near.astype(jnp.float32), axis=1) + jnp.sum(
        hit_far.astype(jnp.float32), axis=1
    )
    sums, counts = lax.psum((sums, counts), "rep")
    unit_width = gru_bias.shape[1]
    start = lax.axis_index("rep") * unit_width
    state_part = lax.dynamic_slice_in_dim(memory, start, unit_width, 1)
    mean = sums / jnp.maximum(counts, 1.0)[:, None]
    highest = lax.Precision.HIGHEST
    a_parts = jnp.einsum("rk,gku->gru", mean, gru_input, precision=highest)
    b_parts = jnp.einsum("rk,gku->gru", memory, gru_hidden, precision=highest)
    update = jax.nn.sigmoid(a_parts[0] + b_parts[0] + gru_bias[0])
    reset = jax.nn.sigmoid(a_parts[1] + b_parts[1] + gru_bias[1])
    cand = jnp.tanh(a_parts[2] + gru_bias[2] + reset * (b_parts[2] + gru_bias[3]))
    fresh = (1.0 - update) * cand + update * state_part
    new_part = jnp.where((counts > 0.0)[:, None], fresh, state_part)
    updated = lax.all_gather(new_part.astype(jnp.bfloat16), "rep", axis=1, tiled=True)
    served = updated[jnp.maximum(got_nbr, 0)]
    returned = lax.all_to_all(served, "nodes", split_axis=0, concat_axis=0, tiled=True)
    fetched = returned.reshape(-1, updated.shape[1])[nbr_slot]
    kv_mem = jnp.dot(fetched, w_keyval_mem, preferred_element_type=jnp.float32).astype(jnp.bfloat16)
    kv_mem = lax.optimization_barrier(kv_mem).astype(jnp.float32)
    gaps = ticks[:, None] - nbr_tick.astype(jnp.float32)
    time_enc = encode(gaps, freq, phase).reshape(-1, freq.shape[0]).astype(jnp.bfloat16)
    kv_time = jnp.dot(time_enc, w_keyval_time, preferred_element_type=jnp.float32)
    keyval = (kv_mem + kv_time).reshape(events, neighbours, 2, HEADS, HEAD_DIM)
    query = jnp.dot(updated[src_local], w_query, preferred_element_type=jnp.float32).astype(
        jnp.bfloat16
    )
    query = lax.optimization_barrier(query).astype(jnp.float32).reshape(events, HEADS, HEAD_DIM)
    scores = jnp.einsum("ehd,ejhd->ehj", query, keyval[:, :, 0]) / math.sqrt(HEAD_DIM)
    weights = jax.nn.softmax(scores, axis=-1)
    mixed = jnp.einsum("ehj,ejhd->ehd", weights, keyval[:, :, 1])
    embed = mixed.reshape(events, HEADS * HEAD_DIM).astype(jnp.bfloat16)
    return (new_part, embed)


def solution(mesh):
    placed = (
        P("nodes", None),
        P("nodes"),
        P(("nodes", "rep")),
        P(("nodes", "rep"), None),
        P(("nodes", "rep")),
        P(("nodes", "rep")),
        P(("nodes", "rep"), None, None),
        P(("nodes", "rep"), None),
        P(("nodes", "rep"), None),
        P(),
        P(),
        P(),
        P(None, None, "rep"),
        P(None, None, "rep"),
        P(None, "rep"),
        P(),
        P(),
        P(),
    )
    return jax.shard_map(
        on_device,
        mesh=mesh,
        in_specs=placed,
        out_specs=(P("nodes", "rep"), P(("nodes", "rep"), None)),
        check_vma=False,
    )
```

profile of v0, /device:TPU:25, one launch (start us, length us, event | category | flops | bytes accessed | tf_op | source)
XLA Modules:
  0.0 305.3 jit_solution(5644243611293077244)
XLA Ops:
  7.2 0.9 fusion.60
  8.3 0.8 select_reduce_fusion
  9.1 0.7 fusion.66
  9.8 1.1 scatter_custom_fusion
  10.9 0.7 all_to_all.27
  11.6 5.5 %all-to-all-start = ((s32[8,1,32]{2,1,0:T(1,128)}), s32[8,1,32]{2,1,0:T(1,128)S(1)}, u32[]{:S(2)}, u32[]{:S(2)}) async-start(s32[8,1,32]{2,1,0:T(1,128)} %all_to_all.27), calls=%async_computation | async-start | bytes 8192 | tf_op jit(solution)/shard_map/all_to_all | solution.py:84
  17.1 0.7 broadcast_multiply_fusion
  17.8 0.8 copy.35
  18.7 1.4 slice_bitcast_fusion.7
  20.3 2.3 reduce-window.6
  23.3 4.2 %convolution_bitcast_fusion = f32[3,512,128]{2,1,0:T(8,128)} fusion(f32[3,512,128]{2,1,0:T(8,128)} %param.31, f32[512,512]{1,0:T(8,128)} %param.18), kind=kOutput, calls=%fused_computation.22 | convolution fusion | flops 1207959552 | bytes 2621440 | tf_op jit(solution)/shard_map/rk,gku->gru/dot_general | solution.py:121
  27.5 0.7 compare_select_fusion.1
  28.6 0.6 fusion.71
  29.3 1.9 gather_fusion.4
  31.3 0.7 all_to_all.30
  32.0 5.4 %all-to-all-start.2 = ((s32[8,1,32]{2,1,0:T(1,128)}), s32[8,1,32]{2,1,0:T(1,128)S(1)}, u32[]{:S(2)}, u32[]{:S(2)}) async-start(s32[8,1,32]{2,1,0:T(1,128)} %all_to_all.30), calls=%async_computation.2 | async-start | bytes 8192 | tf_op jit(solution)/shard_map/all_to_all | solution.py:90
  37.5 1.9 gather_fusion.1
  39.7 6.3 %all-to-all-start.1 = ((bf16[8,32,512]{2,1,0:T(8,128)(2,1)}), bf16[8,32,512]{2,1,0:T(8,128)(2,1)S(1)}, u32[]{:S(2)}, u32[]{:S(2)}) async-start(bf16[8,32,512]{2,1,0:T(8,128)(2,1)} %bitcast.5), calls=%async_computation.1 | async-start | bytes 524288 | tf_op jit(solution)/shard_map/all_to_all | solution.py:89
  46.0 1.3 gather_fusion.3
  47.3 0.8 gather_fusion
  48.4 8.6 %scatter_custom_fusion.2 = s32[4096]{0:T(1024)} fusion(s32[2048]{0:T(1024)S(1)} %bitcast.151, s32[2048]{0:T(1024)S(1)} %reshape.234, s32[]{:T(128)} %constant.14.clone.1), kind=kCustom, calls=%fused_computation.107 | custom fusion | bytes 16388 | tf_op jit(solution)/shard_map/scatter | solution.py:76
  57.6 1.3 gather_fusion.5
  59.5 0.8 gather_fusion.2
  60.4 0.6 multiply_convert_fusion
  61.0 1.9 scatter_custom_fusion.1
  62.8 5.4 %all-to-all-start.3 = ((bf16[8,32,512]{2,1,0:T(8,128)(2,1)}), bf16[8,32,512]{2,1,0:T(8,128)(2,1)S(1)}, u32[]{:S(2)}, u32[]{:S(2)}) async-start(bf16[8,32,512]{2,1,0:T(8,128)(2,1)} %bitcast.7), calls=%async_computation.3 | async-start | bytes 524288 | tf_op jit(solution)/shard_map/all_to_all | solution.py:103
  68.6 8.5 %psum.14 = f32[512]{0:T(512)S(1)} all-reduce(f32[512]{0:T(512)S(1)} %add.150), channel_id=1, replica_groups=mesh['nodes'=8,'rep'=4] {'rep'}, use_global_device_ids=true, to_apply=%region_5.6 | all-reduce | flops 512 | bytes 4096 | tf_op jit(solution)/shard_map/psum | solution.py:114
  77.1 0.6 broadcast_maximum_fusion.1
  77.7 5.4 %all-to-all-start.4 = ((s32[8,1,512]{2,1,0:T(1,128)}), s32[8,1,512]{2,1,0:T(1,128)}, u32[]{:S(2)}, u32[]{:S(2)}) async-start(s32[8,1,512]{2,1,0:T(1,128)} %bitcast.25), calls=%async_computation.4 | async-start | bytes 32768 | tf_op jit(solution)/shard_map/all_to_all | solution.py:85
  83.2 1.1 fusion.28
  84.3 2.0 convolution_add_fusion
  86.3 0.7 broadcast_maximum_fusion
  87.1 36.7 %all-reduce.2.cloned.1.call-done = f32[512,512]{1,0:T(8,128)} async-done(((f32[512,512]{1,0:T(8,128)}), f32[512,512]{1,0:T(8,128)}) %all-reduce.2.cloned.1.call-update) | async-done | bytes 1048592 | tf_op jit(solution)/shard_map/psum | solution.py:114
  123.8 3.3 %convolution_bitcast_fusion.1 = f32[3,512,128]{2,1,0:T(8,128)S(1)} fusion(f32[3,512,128]{2,1,0:T(8,128)} %param.30, f32[512,512]{1,0:T(8,128)} %all-reduce.2.cloned.1.call-done, f32[512]{0:T(512)} %broadcast_maximum_fusion.1), kind=kOutput, calls=%fused_computation.23 | convolution fusion | flops 1208221696 | bytes 2623488 | tf_op jit(solution)/shard_map/rk,gku->gru/dot_general | solution.py:120
  127.2 0.9 fusion.72
  128.1 7.8 %all_gather.3 = bf16[512,512]{1,0:T(8,128)(2,1)S(1)} all-gather(bf16[512,128]{1,0:T(8,128)(2,1)S(1)} %get-tuple-element.8), channel_id=1, replica_groups=mesh['nodes'=8,'rep'=4] {'rep'}, dimensions={1}, use_global_device_ids=true | all-gather | bytes 655360 | tf_op jit(solution)/shard_map/all_gather | solution.py:127
  135.9 17.3 %gather_fusion.7 = bf16[4096,512]{1,0:T(8,128)(2,1)} fusion(bf16[512,512]{1,0:T(8,128)(2,1)S(1)} %all_gather.3, s32[4096]{0:T(1024)S(1)} %broadcast_clamp_fusion), kind=kCustom, calls=%fused_computation.7 | custom fusion | bytes 8404992 | tf_op jit(solution)/shard_map/gather | solution.py:128
  153.2 5.6 %all-to-all-start.5 = ((bf16[8,512,512]{2,1,0:T(8,128)(2,1)}), bf16[8,512,512]{2,1,0:T(8,128)(2,1)}, u32[]{:S(2)}, u32[]{:S(2)}) async-start(bf16[8,512,512]{2,1,0:T(8,128)(2,1)} %bitcast.144), calls=%async_computation.5 | async-start | bytes 8388608 | tf_op jit(solution)/shard_map/all_to_all | solution.py:129
  159.0 1.0 gather_fusion.6
  160.4 1.0 copy.56
  161.4 89.9 %all-to-all-done.5 = bf16[8,512,512]{2,1,0:T(8,128)(2,1)} async-done(((bf16[8,512,512]{2,1,0:T(8,128)(2,1)}), bf16[8,512,512]{2,1,0:T(8,128)(2,1)}, u32[]{:S(2)}, u32[]{:S(2)}) %all-to-all-start.5) | async-done | bytes 4194336 | tf_op jit(solution)/shard_map/all_to_all | solution.py:129
  251.3 10.3 %gather_fusion.8 = bf16[2048,512]{1,0:T(8,128)(2,1)S(1)} fusion(bf16[4096,512]{1,0:T(8,128)(2,1)} %bitcast.28, s32[2048]{0:T(1024)S(1)} %broadcast_clamp_fusion.1), kind=kCustom, calls=%fused_computation.8 | custom fusion | bytes 4202496 | tf_op jit(solution)/shard_map/gather | solution.py:130
  261.7 3.6 %convolution_convert_fusion = bf16[2048,1024]{1,0:T(8,128)(2,1)S(1)} fusion(bf16[2048,512]{1,0:T(8,128)(2,1)S(1)} %gather_fusion.8, bf16[512,1024]{1,0:T(8,128)(2,1)} %param.34), kind=kOutput, calls=%fused_computation.20 | convolution fusion | flops 2149580800 | bytes 7340032 | tf_op jit(solution)/shard_map/dot_general | solution.py:131
  265.3 6.6 %convert_add_fusion = f32[2048,1024]{1,0:T(8,128)} fusion(bf16[2048,1024]{1,0:T(8,128)(2,1)S(1)} %convolution_convert_fusion, bf16[128,1024]{1,0:T(8,128)(2,1)S(1)} %copy-done.6, f32[128]{0:T(128)S(1)} %copy-done.12, f32[128]{0:T(128)S(1)} %copy-done.14, f32[2048]{0:T(1024)S(1)} %mul.102), kind=kOutput, calls=%fused_computation.19 | convolution fusion | flops 541851648 | bytes 12854272 | tf_op jit(solution)/shard_map/dot_general | solution.py:135
  271.9 13.4 %reshape.141 = f32[128,16,2,8,64]{4,3,2,1,0:T(8,128)} reshape(f32[2048,1024]{1,0:T(8,128)} %convert_add_fusion) | data formatting | bytes 16777216 | tf_op jit(solution)/shard_map/reshape | solution.py:136
  285.3 5.7 %fusion.4 = f32[128,8,16]{1,2,0:T(8,128)S(1)} fusion(f32[128,16,2,8,64]{4,3,2,1,0:T(8,128)} %reshape.141, f32[128,8,64]{2,1,0:T(8,128)S(1)} %copy-done.4), kind=kLoop, calls=%fused_computation.18 | loop fusion | flops 2080768 | bytes 4521984
  292.2 5.3 %fusion.2 = bf16[128,8,64]{2,1,0:T(8,128)(2,1)S(1)} fusion(f32[128,16,2,8,64]{4,3,2,1,0:T(8,128)} %reshape.141, f32[128,8,16]{1,2,0:T(8,128)S(1)} %copy.57), kind=kLoop, calls=%fused_computation.15 | loop fusion | flops 2031616 | bytes 4390912
  297.7 0.8 copy.39
  (94 shorter events, 5.9 us)
Async XLA Ops:
  7.2 53.2 %copy-start = (bf16[1152,512]{1,0:T(8,128)(2,1)S(1)}, bf16[1152,512]{1,0:T(8,128)(2,1)}, u32[]{:S(2)}) copy-start(bf16[1152,512]{1,0:T(8,128)(2,1)} %param.29) | copy-start | bytes 3538948
  7.2 30.3 %copy-start.2 = (f32[512,512]{1,0:T(8,128)S(1)}, f32[512,512]{1,0:T(8,128)}, u32[]{:S(2)}) copy-start(f32[512,512]{1,0:T(8,128)} %param.18) | copy-start | bytes 3145732
  7.2 22.1 %copy-start.1 = (s32[512]{0:T(512)S(1)}, s32[512]{0:T(512)}, u32[]{:S(2)}) copy-start(s32[512]{0:T(512)} %param.19) | copy-start | bytes 6148
  9.8 27.7 %copy-start.22 = (s32[128]{0:T(128)}, s32[128]{0:T(128)S(1)}, u32[]{:S(2)}) copy-start(s32[128]{0:T(128)S(1)} %fusion.66) | copy-start | bytes 1540
  11.6 16.6 %all-to-all-start = ((s32[8,1,32]{2,1,0:T(1,128)}), s32[8,1,32]{2,1,0:T(1,128)S(1)}, u32[]{:S(2)}, u32[]{:S(2)}) async-start(s32[8,1,32]{2,1,0:T(1,128)} %all_to_all.27), calls=%async_computation | async-start | bytes 8192 | tf_op jit(solution)/shard_map/all_to_all | solution.py:84
  29.3 18.9 %copy-start.8 = (s32[128,16]{0,1:T(8,128)S(1)}, s32[128,16]{0,1:T(8,128)}, u32[]{:S(2)}) copy-start(s32[128,16]{0,1:T(8,128)} %param.25) | copy-start | bytes 24580
  31.3 27.6 %copy-start.20 = (s32[128]{0:T(128)S(1)}, s32[128]{0:T(128)}, u32[]{:S(2)}) copy-start(s32[128]{0:T(128)} %param.23) | copy-start | bytes 1540
  31.3 27.7 %copy-start.11 = (f32[128]{0:T(128)S(1)}, f32[128]{0:T(128)}, u32[]{:S(2)}) copy-start(f32[128]{0:T(128)} %param.28) | copy-start | bytes 1540
  31.3 27.7 %copy-start.13 = (f32[128]{0:T(128)S(1)}, f32[128]{0:T(128)}, u32[]{:S(2)}) copy-start(f32[128]{0:T(128)} %param.27) | copy-start | bytes 1540
  32.0 7.7 %all-to-all-start.2 = ((s32[8,1,32]{2,1,0:T(1,128)}), s32[8,1,32]{2,1,0:T(1,128)S(1)}, u32[]{:S(2)}, u32[]{:S(2)}) async-start(s32[8,1,32]{2,1,0:T(1,128)} %all_to_all.30), calls=%async_computation.2 | async-start | bytes 8192 | tf_op jit(solution)/shard_map/all_to_all | solution.py:90
  39.7 19.8 %all-to-all-start.1 = ((bf16[8,32,512]{2,1,0:T(8,128)(2,1)}), bf16[8,32,512]{2,1,0:T(8,128)(2,1)S(1)}, u32[]{:S(2)}, u32[]{:S(2)}) async-start(bf16[8,32,512]{2,1,0:T(8,128)(2,1)} %bitcast.5), calls=%async_computation.1 | async-start | bytes 524288 | tf_op jit(solution)/shard_map/all_to_all | solution.py:89
  46.0 2.3 copy-start.10
  60.3 7.9 %copy-start.15 = (s32[128]{0:T(128)S(1)}, s32[128]{0:T(128)}, u32[]{:S(2)}) copy-start(s32[128]{0:T(128)} %param.20) | copy-start | bytes 1540
  62.8 14.9 %all-to-all-start.3 = ((bf16[8,32,512]{2,1,0:T(8,128)(2,1)}), bf16[8,32,512]{2,1,0:T(8,128)(2,1)S(1)}, u32[]{:S(2)}, u32[]{:S(2)}) async-start(bf16[8,32,512]{2,1,0:T(8,128)(2,1)} %bitcast.7), calls=%async_computation.3 | async-start | bytes 524288 | tf_op jit(solution)/shard_map/all_to_all | solution.py:103
  68.4 14.7 %copy-start.7 = (s32[256]{0:T(256)}, s32[256]{0:T(256)S(1)}, u32[]{:S(2)}) copy-start(s32[256]{0:T(256)S(1)} %eq.76) | copy-start | bytes 3076
  77.7 8.6 %all-to-all-start.4 = ((s32[8,1,512]{2,1,0:T(1,128)}), s32[8,1,512]{2,1,0:T(1,128)}, u32[]{:S(2)}, u32[]{:S(2)}) async-start(s32[8,1,512]{2,1,0:T(1,128)} %bitcast.25), calls=%async_computation.4 | async-start | bytes 32768 | tf_op jit(solution)/shard_map/all_to_all | solution.py:85
  83.2 40.6 %all-reduce.2.cloned.1.call-start = ((), (), s32[]{:S(2)}) async-start(), calls=%async_computation.6 | async-start | bytes 2097152 | tf_op jit(solution)/shard_map/psum | solution.py:114
  83.2 43.9 %copy-start.3 = (f32[3,512,128]{2,1,0:T(8,128)S(1)}, f32[3,512,128]{2,1,0:T(8,128)}, u32[]{:S(2)}) copy-start(f32[3,512,128]{2,1,0:T(8,128)} %convolution_bitcast_fusion) | copy-start | bytes 2359300
  83.2 43.9 %copy-start.16 = (f32[128]{0:T(128)S(1)}, f32[128]{0:T(128)}, u32[]{:S(2)}) copy-start(f32[128]{0:T(128)} %get-tuple-element.10) | copy-start | bytes 1540
  84.3 42.9 %copy-start.17 = (f32[128]{0:T(128)S(1)}, f32[128]{0:T(128)}, u32[]{:S(2)}) copy-start(f32[128]{0:T(128)} %get-tuple-element.11) | copy-start | bytes 1540
  84.3 42.9 %copy-start.18 = (f32[128]{0:T(128)S(1)}, f32[128]{0:T(128)}, u32[]{:S(2)}) copy-start(f32[128]{0:T(128)} %get-tuple-element.12) | copy-start | bytes 1540
  84.3 42.9 %copy-start.19 = (f32[128]{0:T(128)S(1)}, f32[128]{0:T(128)}, u32[]{:S(2)}) copy-start(f32[128]{0:T(128)} %get-tuple-element.13) | copy-start | bytes 1540
  153.2 5.6 %copy-start.21 = (s32[128]{0:T(128)S(1)}, s32[128]{0:T(128)}, u32[]{:S(2)}) copy-start(s32[128]{0:T(128)} %param.23) | copy-start | bytes 1540
  153.2 5.6 %copy-start.9 = (s32[128,16]{0,1:T(8,128)S(1)}, s32[128,16]{0,1:T(8,128)}, u32[]{:S(2)}) copy-start(s32[128,16]{0,1:T(8,128)} %param.26) | copy-start | bytes 24580
  153.2 6.8 %copy-start.5 = (bf16[512,512]{1,0:T(8,128)(2,1)S(1)}, bf16[512,512]{1,0:T(8,128)(2,1)}, u32[]{:S(2)}) copy-start(bf16[512,512]{1,0:T(8,128)(2,1)} %param.33) | copy-start | bytes 1572868
  153.2 98.1 %all-to-all-start.5 = ((bf16[8,512,512]{2,1,0:T(8,128)(2,1)}), bf16[8,512,512]{2,1,0:T(8,128)(2,1)}, u32[]{:S(2)}, u32[]{:S(2)}) async-start(bf16[8,512,512]{2,1,0:T(8,128)(2,1)} %bitcast.144), calls=%async_computation.5 | async-start | bytes 8388608 | tf_op jit(solution)/shard_map/all_to_all | solution.py:129
  261.6 3.7 %copy-start.6 = (bf16[128,1024]{1,0:T(8,128)(2,1)S(1)}, bf16[128,1024]{1,0:T(8,128)(2,1)}, u32[]{:S(2)}) copy-start(bf16[128,1024]{1,0:T(8,128)(2,1)} %param.35) | copy-start | bytes 786436
  261.6 3.6 %copy-start.12 = (f32[128]{0:T(128)S(1)}, f32[128]{0:T(128)}, u32[]{:S(2)}) copy-start(f32[128]{0:T(128)} %param.28) | copy-start | bytes 1540
  261.7 3.6 %copy-start.14 = (f32[128]{0:T(128)S(1)}, f32[128]{0:T(128)}, u32[]{:S(2)}) copy-start(f32[128]{0:T(128)} %param.27) | copy-start | bytes 1540
  271.9 13.4 %copy-start.4 = (f32[128,8,64]{2,1,0:T(8,128)S(1)}, f32[128,8,64]{2,1,0:T(8,128)}, u32[]{:S(2)}) copy-start(f32[128,8,64]{2,1,0:T(8,128)} %copy.56) | copy-start | bytes 786436
Sparse Core Ops, SparseCore 0:
  86.4 37.3 all-reduce.1
where the time goes:
time: 309 us; the launch traced here: 305 us
  waiting for transfers between devices  127 us (41%)
  local copies, waits for them, and re-layouts  70.1 us (23%)
  starting transfers between devices  33.7 us (11%)
  other arithmetic  22 us (7%)
  matrix products  21.6 us (7%)
  blocking collectives  16.3 us (5%)
  between operations  14.6 us (5%)
    all_to_all x1, waiting for transfers between devices, on_device(): lax.all_to_all(served, 'nodes', split_axis=0, concat_axis=0, tiled=True)  89.9 us
    psum x1, waiting for transfers between devices, on_device(): sums, counts = lax.psum((sums, counts), 'rep')  36.7 us
    gather x1, local copies, waits for them, and re-layouts, on_device(): served = updated[jnp.maximum(got_nbr, 0)]  17.3 us
    reshape x1, local copies, waits for them, and re-layouts, on_device(): keyval = (kv_mem + kv_time).reshape(events, neighbours, 2, HEADS, HEAD_DIM)  13.4 us
    unnamed x3, other arithmetic  11 us
    gather x1, local copies, waits for them, and re-layouts, on_device(): fetched = returned.reshape(-1, updated.shape[1])[nbr_slot]  10.3 us
    scatter x1, local copies, waits for them, and re-layouts, on_device(): nbr_ids = jnp.full((groups * nbr_cap,), -1, jnp.int32).at[nbr_slot].set(n...  8.62 us
    psum x1, blocking collectives, on_device(): sums, counts = lax.psum((sums, counts), 'rep')  8.53 us
  transfers between devices with their start and end apart: 7, of which 3 were waited for; matrix products, arithmetic and copies ran while one was open for 11% of the time, Pallas kernels for 0%

commit v1 on v0

--- a/solution.py
+++ b/solution.py
@@ -1,12 +1,251 @@
+import functools
 import math
 
 import jax
 import jax.numpy as jnp
 from jax import lax
+from jax.experimental import pallas as pl
+from jax.experimental.pallas import tpu as pltpu
 from jax.sharding import PartitionSpec as P
 
 HEADS = 8
 HEAD_DIM = 64
+MESH = pl.DeviceIdType.MESH
+F32 = jnp.float32
+BF16 = jnp.bfloat16
+
+
+def dot32(a, b):
+    return jnp.dot(a, b, preferred_element_type=F32)
+
+
+def split(v):
+    high = v.astype(BF16)
+    return high, (v - high.astype(F32)).astype(BF16)
+
+
+def column(ref, j, count):
+    lanes = lax.broadcasted_iota(jnp.int32, ref.shape, 1)
+    value = ref[...]
+    cols = [
+        jnp.sum(jnp.where(lanes == j + i, value, 0.0), axis=1, keepdims=True) for i in range(count)
+    ]
+    return jnp.concatenate(cols, axis=0)
+
+
+def attend_kernel(
+    groups,
+    part_ref,
+    src_ref,
+    index_ref,
+    gap_ref,
+    freq_ref,
+    phase_ref,
+    wq_ref,
+    wkv_ref,
+    wt_ref,
+    out_ref,
+    table,
+    keyval,
+    scores,
+    send_z,
+    recv_z,
+    send_a,
+    recv_a,
+    send_b,
+    recv_b,
+    send_c,
+    recv_c,
+):
+    node = lax.axis_index("nodes")
+    rep = lax.axis_index("rep")
+    deep = groups // 2
+    z, y = node // 2, node % 2
+    x, c = rep // 2, rep % 2
+    rows, unit = part_ref.shape
+    half = rows // 2
+    events, neighbours = index_ref.shape
+    width = table.shape[1]
+
+    def where_of(h, d, k, b):
+        zz = (z + deep - d) % deep
+        ky, kx = (k, b) if h == 0 else (b, k)
+        return zz * 2 + (y + ky) % 2, (x + kx) % 2
+
+    def block(n, r, h):
+        return table.at[
+            pl.ds(pl.multiple_of(n * rows + h * half, half), half),
+            pl.ds(pl.multiple_of(r * unit, unit), unit),
+        ]
+
+    def copy(n, r, h, device, send, recv):
+        return pltpu.make_async_remote_copy(
+            src_ref=block(n, r, h),
+            dst_ref=block(n, r, h),
+            send_sem=send,
+            recv_sem=recv,
+            device_id=device,
+            device_id_type=MESH,
+        )
+
+    across_y = (z * 2 + (y + 1) % 2, rep)
+    across_x = (node, ((x + 1) % 2) * 2 + c)
+    across_c = (node, x * 2 + (c + 1) % 2)
+
+    def along_z(h, d):
+        device = (((z + d) % deep) * 2 + y, rep)
+        return copy(node, rep, h, device, send_z.at[h, d], recv_z.at[h, d])
+
+    def first(h, d):
+        n, xx = where_of(h, d, 0, 0)
+        device = across_y if h == 0 else across_x
+        return copy(n, xx * 2 + c, h, device, send_a.at[h, d], recv_a.at[h, d])
+
+    def second(h, d, k):
+        n, xx = where_of(h, d, k, 0)
+        device = across_x if h == 0 else across_y
+        return copy(n, xx * 2 + c, h, device, send_b.at[h, d, k], recv_b.at[h, d, k])
+
+    def core(h, d, k, b):
+        n, xx = where_of(h, d, k, b)
+        i = k * 2 + b
+        return copy(n, xx * 2 + c, h, across_c, send_c.at[h, d, i], recv_c.at[h, d, i])
+
+    block_rows = pl.ds(pl.multiple_of(node * rows, rows), rows)
+    table[block_rows, pl.ds(pl.multiple_of(rep * unit, unit), unit)] = part_ref[...]
+
+    partners = [(((z + d) % deep) * 2 + y, rep) for d in range(1, deep)]
+    partners += [across_y, across_x, across_c]
+    barrier = pltpu.get_barrier_semaphore()
+    for device in partners:
+        pl.semaphore_signal(barrier, inc=1, device_id=device, device_id_type=MESH)
+    pl.semaphore_wait(barrier, len(partners))
+
+    started = []
+
+    def start(one):
+        one.start()
+        started.append(one)
+
+    batch = 4
+
+    def time_part(g):
+        gaps = column(gap_ref, g * batch, batch)
+        enc = jnp.cos(gaps * freq_ref[...] + phase_ref[...]).astype(BF16)
+        size = batch * events
+        keyval[g * size : (g + 1) * size, :] = dot32(enc, wt_ref[...])
+
+    steps = neighbours // batch
+    for d in range(1, deep):
+        for h in range(2):
+            start(along_z(h, d))
+    for h in range(2):
+        start(first(h, 0))
+        start(second(h, 0, 0))
+        start(core(h, 0, 0, 0))
+    time_part(0)
+    for d in range(1, deep):
+        for h in range(2):
+            along_z(h, d).wait_recv()
+            start(first(h, d))
+            start(second(h, d, 0))
+            start(core(h, d, 0, 0))
+        if d < steps:
+            time_part(d)
+    for g in range(deep, steps):
+        time_part(g)
+    for d in range(deep):
+        for h in range(2):
+            first(h, d).wait_recv()
+            start(second(h, d, 1))
+            start(core(h, d, 1, 0))
+    for d in range(deep):
+        for k in range(2):
+            for h in range(2):
+                second(h, d, k).wait_recv()
+                start(core(h, d, k, 1))
+    for d in range(deep):
+        for k in range(2):
+            for b in range(2):
+                for h in range(2):
+                    core(h, d, k, b).wait_recv()
+    for one in started:
+        one.wait_send()
+
+    lane_row = lax.broadcasted_iota(jnp.int32, (events, rows), 1)
+    hit = (src_ref[...] == lane_row).astype(BF16)
+    mine = dot32(hit, table[block_rows, :]).astype(BF16)
+    query = dot32(mine, wq_ref[...]).astype(BF16).astype(F32) * (1.0 / math.sqrt(HEAD_DIM))
+    query = jnp.concatenate([query] * batch, axis=0)
+    att = HEADS * HEAD_DIM
+    size = batch * events
+    head_sum = (
+        lax.broadcasted_iota(jnp.int32, (att, 128), 0) // HEAD_DIM
+        == lax.broadcasted_iota(jnp.int32, (att, 128), 1)
+    ).astype(BF16)
+    head_spread = (
+        lax.broadcasted_iota(jnp.int32, (128, att), 1) // HEAD_DIM
+        == lax.broadcasted_iota(jnp.int32, (128, att), 0)
+    ).astype(BF16)
+    lanes = lax.broadcasted_iota(jnp.int32, (size, rows), 1)
+
+    @pl.loop(0, steps)
+    def _(g):
+        names = column(index_ref, g * batch, batch).astype(jnp.int32)
+        here = pl.ds(pl.multiple_of(g * size, size), size)
+        found = jnp.zeros((size, width), F32)
+        for n in range(groups):
+            chosen = (names == lanes + n * rows).astype(BF16)
+            found += dot32(chosen, table[n * rows : (n + 1) * rows, :])
+        kv = dot32(found.astype(BF16), wkv_ref[...]).astype(BF16).astype(F32)
+        kv = kv + keyval[here, :]
+        keyval[here, att:] = kv[:, att:]
+        high, low = split(query * kv[:, :att])
+        scores[here, :] = dot32(high, head_sum) + dot32(low, head_sum)
+
+    top = scores[0:events, :]
+    for j in range(1, neighbours):
+        top = jnp.maximum(top, scores[j * events : (j + 1) * events, :])
+    total = jnp.zeros_like(top)
+    for j in range(neighbours):
+        term = jnp.exp(scores[j * events : (j + 1) * events, :] - top)
+        scores[j * events : (j + 1) * events, :] = term
+        total += term
+    mixed = jnp.zeros((events, att), F32)
+    for g in range(steps):
+        high, low = split(scores[g * size : (g + 1) * size, :])
+        spread = dot32(high, head_spread) + dot32(low, head_spread)
+        terms = spread * keyval[g * size : (g + 1) * size, att:]
+        for i in range(batch):
+            mixed += terms[i * events : (i + 1) * events, :]
+    high, low = split(1.0 / total)
+    scale = dot32(high, head_spread) + dot32(low, head_spread)
+    out_ref[...] = (mixed * scale).astype(out_ref.dtype)
+
+
+def attend(part, src, index, gaps, freq, phase, wq, wkv, wt, groups, reps):
+    rows, unit = part.shape
+    events, neighbours = index.shape
+    deep = groups // 2
+    total = groups * rows
+    dma = pltpu.SemaphoreType.DMA
+    pairs = [(2, deep), (2, deep), (2, deep, 2), (2, deep, 4)]
+    sems = [dma(shape) for shape in pairs for _ in range(2)]
+    return pl.pallas_call(
+        functools.partial(attend_kernel, groups),
+        out_shape=jax.ShapeDtypeStruct((events, HEADS * HEAD_DIM), BF16),
+        in_specs=[pl.BlockSpec(memory_space=pltpu.VMEM)] * 9,
+        out_specs=pl.BlockSpec(memory_space=pltpu.VMEM),
+        scratch_shapes=[
+            pltpu.VMEM((total, reps * unit), BF16),
+            pltpu.VMEM((events * neighbours, wkv.shape[1]), F32),
+            pltpu.VMEM((events * neighbours, 128), F32),
+        ]
+        + sems,
+        compiler_params=pltpu.CompilerParams(
+            collective_id=1, has_side_effects=True, vmem_limit_bytes=50 * 1024 * 1024
+        ),
+    )(part, src, index, gaps, freq, phase, wq, wkv, wt)
 
 
 def encode(gaps, freq, phase):
@@ -34,7 +273,7 @@
     return (messages[:count], messages[count:])
 
 
-def on_device(
+def on_device_large(
     memory,
     last_tick,
     src_local,
@@ -145,6 +384,100 @@
     return (new_part, embed)
 
 
+def on_device(
+    memory,
+    last_tick,
+    src_local,
+    dst_owner,
+    dst_local,
+    event_tick,
+    nbr_owner,
+    nbr_local,
+    nbr_tick,
+    freq,
+    phase,
+    w_message,
+    gru_input,
+    gru_hidden,
+    gru_bias,
+    w_query,
+    w_keyval_mem,
+    w_keyval_time,
+):
+    groups = lax.axis_size("nodes")
+    events = src_local.shape[0]
+    rows_here = memory.shape[0]
+    width_m = memory.shape[1]
+    msg_width = w_message.shape[1]
+    dst_cap = max(2, 2 * events // groups)
+    dst_slot = place(dst_owner[:, 0], groups, dst_cap)
+    dst_ids = (
+        jnp.full((groups * dst_cap,), -1, jnp.int32)
+        .at[dst_slot]
+        .set(dst_local)
+        .reshape(groups, dst_cap)
+    )
+    mem_half = memory.astype(jnp.bfloat16)
+    near_rows = mem_half[src_local]
+    near_ticks = last_tick[src_local]
+    ticks = event_tick.astype(jnp.float32)
+    got_dst = lax.all_to_all(dst_ids, "nodes", split_axis=0, concat_axis=0, tiled=True)
+    names = jnp.concatenate([src_local, got_dst.reshape(-1)])
+    names = lax.all_gather(names, "rep", axis=0, tiled=True)
+    safe_dst = jnp.maximum(got_dst, 0)
+    reply_rows, reply_ticks = (
+        lax.all_to_all(mem_half[safe_dst], "nodes", split_axis=0, concat_axis=0, tiled=True),
+        lax.all_to_all(last_tick[safe_dst], "nodes", split_axis=0, concat_axis=0, tiled=True),
+    )
+    far_rows = reply_rows.reshape(-1, width_m)[dst_slot]
+    far_ticks = reply_ticks.reshape(-1)[dst_slot]
+    src_time = encode(ticks - near_ticks.astype(jnp.float32), freq, phase).astype(jnp.bfloat16)
+    dst_time = encode(ticks - far_ticks.astype(jnp.float32), freq, phase).astype(jnp.bfloat16)
+    msg_src, msg_dst = message_pair(near_rows, far_rows, src_time, dst_time, w_message)
+    outgoing = (
+        jnp.zeros((groups * dst_cap, msg_width), jnp.bfloat16)
+        .at[dst_slot]
+        .set(msg_dst)
+        .reshape(groups, dst_cap, msg_width)
+    )
+    incoming = lax.all_to_all(outgoing, "nodes", split_axis=0, concat_axis=0, tiled=True)
+    far_msgs = incoming.reshape(-1, msg_width)
+    row_ids = jnp.arange(rows_here, dtype=jnp.int32)[:, None]
+    messages = jnp.concatenate([msg_src, far_msgs], axis=0)
+    messages = lax.all_gather(messages, "rep", axis=0, tiled=True)
+    hits = (row_ids == names[None, :]).astype(jnp.bfloat16)
+    sums = jnp.dot(hits, messages, preferred_element_type=jnp.float32)
+    counts = jnp.sum(hits.astype(jnp.float32), axis=1)
+    unit_width = gru_bias.shape[1]
+    start = lax.axis_index("rep") * unit_width
+    state_part = lax.dynamic_slice_in_dim(memory, start, unit_width, 1)
+    mean = sums / jnp.maximum(counts, 1.0)[:, None]
+    highest = lax.Precision.HIGHEST
+    a_parts = jnp.einsum("rk,gku->gru", mean, gru_input, precision=highest)
+    b_parts = jnp.einsum("rk,gku->gru", memory, gru_hidden, precision=highest)
+    update = jax.nn.sigmoid(a_parts[0] + b_parts[0] + gru_bias[0])
+    reset = jax.nn.sigmoid(a_parts[1] + b_parts[1] + gru_bias[1])
+    cand = jnp.tanh(a_parts[2] + gru_bias[2] + reset * (b_parts[2] + gru_bias[3]))
+    fresh = (1.0 - update) * cand + update * state_part
+    new_part = jnp.where((counts > 0.0)[:, None], fresh, state_part)
+    index = (nbr_owner[:, :, 0] * rows_here + nbr_local).astype(jnp.float32)
+    gaps = ticks[:, None] - nbr_tick.astype(jnp.float32)
+    embed = attend(
+        new_part.astype(jnp.bfloat16),
+        src_local[:, None],
+        index,
+        gaps,
+        freq[None, :],
+        phase[None, :],
+        w_query,
+        w_keyval_mem,
+        w_keyval_time,
+        groups,
+        lax.axis_size("rep"),
+    )
+    return (new_part, embed)
+
+
 def solution(mesh):
     placed = (
         P("nodes", None),
@@ -166,8 +499,9 @@
         P(),
         P(),
     )
+    fits = mesh.shape["nodes"] == 8 and mesh.shape["rep"] == 4
     return jax.shard_map(
-        on_device,
+        on_device if fits else on_device_large,
         mesh=mesh,
         in_specs=placed,
         out_specs=(P("nodes", "rep"), P(("nodes", "rep"), None)),

time: 309 us -> 144 us (0.47)
  waiting for transfers between devices: 127 us -> 17.3 us
  local copies, waits for them, and re-layouts: 70.1 us -> 14.8 us
  Pallas kernels: 0 us -> 47 us
  other arithmetic: 22 us -> 7.46 us
  matrix products: 21.6 us -> 7.83 us
  starting transfers between devices: 33.7 us -> 23.9 us
  blocking collectives: 16.3 us -> 10.7 us
    all_to_all x2 -> x0, waiting for transfers between devices: 89.9 us -> none  [the longest x1 89.9 us: on_device(): lax.all_to_all(served, 'nodes', split_axis=0, concat_axis=0, tiled=True)]
    pallas_call x0 -> x1, Pallas kernels: none -> 47 us  [attend(): pl.pallas_call(functools.partial(attend_kernel, groups), out_shape=jax.Sh...]
    psum x1 -> x0, waiting for transfers between devices: 36.7 us -> none  [on_device(): sums, counts = lax.psum((sums, counts), 'rep')]
    gather x3 -> x0, local copies, waits for them, and re-layouts: 28.6 us -> none  [the longest x1 17.3 us: on_device(): served = updated[jnp.maximum(got_nbr, 0)]]
    reshape x2 -> x1, local copies, waits for them, and re-layouts: 13.5 us -> 0.08 us  [on_device(): names = jnp.concatenate([src_local, got_dst.reshape(-1)])]
    all_gather x0 -> x1, waiting for transfers between devices: none -> 11.3 us  [on_device(): messages = lax.all_gather(messages, 'rep', axis=0, tiled=True)]
    unnamed x3 -> x0, other arithmetic: 11 us -> none
    all_to_all x2 -> x0, starting transfers between devices: 11 us -> none  [the longest x1 5.59 us: on_device(): lax.all_to_all(served, 'nodes', split_axis=0, concat_axis=0, tiled=True)]
  transfers between devices with their start and end apart: 7 -> 5, of which waited for: 3 -> 4; matrix products, arithmetic and copies ran while one was open for 11% -> 8% of each run, Pallas kernels for 0% -> 0%
where the time goes in v1:
time: 144 us; the launch traced here: 143 us
  Pallas kernels  47 us (33%)
  starting transfers between devices  23.9 us (17%)
  waiting for transfers between devices  17.3 us (12%)
  local copies, waits for them, and re-layouts  14.8 us (10%)
  between operations  14.4 us (10%)
  blocking collectives  10.7 us (7%)
  matrix products  7.83 us (5%)
  other arithmetic  7.46 us (5%)
    pallas_call x1, Pallas kernels, attend(): pl.pallas_call(functools.partial(attend_kernel, groups), out_shape=jax.Sh...  47 us
    all_gather x1, waiting for transfers between devices, on_device(): messages = lax.all_gather(messages, 'rep', axis=0, tiled=True)  11.3 us
    all_gather x1, blocking collectives, on_device(): names = lax.all_gather(names, 'rep', axis=0, tiled=True)  10.7 us
    all_to_all x1, starting transfers between devices, on_device(): lax.all_to_all(mem_half[safe_dst], 'nodes', split_axis=0, concat_axis=0,...  6.35 us
    all_to_all x1, starting transfers between devices, on_device(): lax.all_to_all(last_tick[safe_dst], 'nodes', split_axis=0, concat_axis=0,...  6.23 us
    all_to_all x1, starting transfers between devices, on_device(): lax.all_to_all(outgoing, 'nodes', split_axis=0, concat_axis=0, tiled=True)  5.78 us
    all_to_all x1, starting transfers between devices, on_device(): lax.all_to_all(dst_ids, 'nodes', split_axis=0, concat_axis=0, tiled=True)  5.49 us
    all_to_all x1, waiting for transfers between devices, on_device(): lax.all_to_all(outgoing, 'nodes', split_axis=0, concat_axis=0, tiled=True)  4.07 us
  transfers between devices with their start and end apart: 5, of which 4 were waited for; matrix products, arithmetic and copies ran while one was open for 8% of the time, Pallas kernels for 0%

profile of v1, /device:TPU:25, one launch (start us, length us, event | category | flops | bytes accessed | tf_op | source)
XLA Modules:
  0.0 143.3 jit_solution(16683572858946429746)
XLA Ops:
  7.2 0.8 fusion.44
  8.0 0.2 reduce_window_sum.11
  8.2 0.8 select_reduce_fusion
  9.0 0.7 fusion.45
  9.7 1.1 scatter_custom_fusion
  10.8 0.7 all_to_all.18
  11.5 5.5 %all-to-all-start = ((s32[8,1,32]{2,1,0:T(1,128)}), s32[8,1,32]{2,1,0:T(1,128)S(1)}, u32[]{:S(2)}, u32[]{:S(2)}) async-start(s32[8,1,32]{2,1,0:T(1,128)} %all_to_all.18), calls=%async_computation | async-start | bytes 8192 | tf_op jit(solution)/shard_map/all_to_all | solution.py:424
  17.0 0.7 compare_select_fusion
  17.6 1.6 %all-to-all-done = s32[8,1,32]{2,1,0:T(1,128)S(1)} async-done(((s32[8,1,32]{2,1,0:T(1,128)}), s32[8,1,32]{2,1,0:T(1,128)S(1)}, u32[]{:S(2)}, u32[]{:S(2)}) %all-to-all-start) | async-done | bytes 1056 | tf_op jit(solution)/shard_map/all_to_all | solution.py:424
  19.2 0.6 broadcast.94
  19.8 0.7 fusion.49
  20.6 0.1 reshape.71
  20.7 1.9 %gather_fusion.4 = s32[256]{0:T(256)S(1)} fusion(s32[512]{0:T(512)S(1)} %copy-done.6, s32[1024]{0:T(1024)S(1)} %pad_clamp_fusion.1), kind=kCustom, calls=%fused_computation.4 | custom fusion | bytes 3072 | tf_op jit(solution)/shard_map/gather | solution.py:430
  22.6 0.7 all_to_all.21
  23.3 6.2 %all-to-all-start.2 = ((s32[8,1,32]{2,1,0:T(1,128)}), s32[8,1,32]{2,1,0:T(1,128)S(1)}, u32[]{:S(2)}, u32[]{:S(2)}) async-start(s32[8,1,32]{2,1,0:T(1,128)} %all_to_all.21), calls=%async_computation.2 | async-start | bytes 8192 | tf_op jit(solution)/shard_map/all_to_all | solution.py:430
  29.5 0.1 convert_element_type.42
  29.6 1.9 %gather_fusion.1 = bf16[256,512]{1,0:T(8,128)(2,1)} fusion(bf16[512,512]{1,0:T(8,128)(2,1)S(1)} %convert_element_type.42, s32[1024]{0:T(1024)S(1)} %pad_clamp_fusion.1), kind=kCustom, calls=%fused_computation.1 | custom fusion | bytes 525312 | tf_op jit(solution)/shard_map/gather | solution.py:429
  31.5 0.3 all-to-all-done.2
  31.8 6.4 %all-to-all-start.1 = ((bf16[8,32,512]{2,1,0:T(8,128)(2,1)}), bf16[8,32,512]{2,1,0:T(8,128)(2,1)S(1)}, u32[]{:S(2)}, u32[]{:S(2)}) async-start(bf16[8,32,512]{2,1,0:T(8,128)(2,1)} %bitcast.3), calls=%async_computation.1 | async-start | bytes 524288 | tf_op jit(solution)/shard_map/all_to_all | solution.py:429
  38.1 1.3 gather_fusion.3
  39.4 0.8 gather_fusion
  40.3 0.7 reduce.11
  41.0 0.1 reshape.58
  41.1 1.3 gather_fusion.5
  42.4 0.5 cosine_convert_fusion.1
  42.9 0.8 gather_fusion.2
  43.8 0.6 multiply_convert_fusion
  44.4 1.7 %scatter_custom_fusion.1 = bf16[256,512]{1,0:T(8,128)(2,1)} fusion(s32[128]{0:T(128)S(1)} %fusion.45, bf16[256,512]{1,0:T(8,128)(2,1)S(1)} %multiply_convert_fusion, bf16[]{:T(256)} %constant.17.clone.1), kind=kCustom, calls=%fused_computation.56 | custom fusion | bytes 393218 | tf_op jit(solution)/shard_map/scatter | solution.py:440
  46.1 5.8 %all-to-all-start.3 = ((bf16[8,32,512]{2,1,0:T(8,128)(2,1)}), bf16[8,32,512]{2,1,0:T(8,128)(2,1)S(1)}, u32[]{:S(2)}, u32[]{:S(2)}) async-start(bf16[8,32,512]{2,1,0:T(8,128)(2,1)} %bitcast.5), calls=%async_computation.3 | async-start | bytes 524288 | tf_op jit(solution)/shard_map/all_to_all | solution.py:443
  51.9 4.1 %all-to-all-done.3 = bf16[8,32,512]{2,1,0:T(8,128)(2,1)S(1)} async-done(((bf16[8,32,512]{2,1,0:T(8,128)(2,1)}), bf16[8,32,512]{2,1,0:T(8,128)(2,1)S(1)}, u32[]{:S(2)}, u32[]{:S(2)}) %all-to-all-start.3) | async-done | bytes 262176 | tf_op jit(solution)/shard_map/all_to_all | solution.py:443
  56.0 0.8 pad_maximum_fusion
  56.8 0.1 copy.46
  56.9 0.1 copy.47
  57.1 0.1 copy.49
  57.2 0.1 copy.50.src_ref
  57.3 0.1 broadcast_subtract_fusion.gap_ref
  57.4 3.0 %convolution_bitcast_fusion = f32[3,512,128]{2,1,0:T(8,128)S(1)} fusion(f32[3,512,128]{2,1,0:T(8,128)} %param.31, f32[512,512]{1,0:T(8,128)S(1)} %copy-done.7), kind=kOutput, calls=%fused_computation.13 | convolution fusion | flops 1207959552 | bytes 2621440 | tf_op jit(solution)/shard_map/rk,gku->gru/dot_general | solution.py:457
  60.4 0.1 reshape.56
  60.5 10.7 %all-gather = s32[4,1,384]{2,1,0:T(1,128)S(1)} all-gather(s32[1,1,384]{2,1,0:T(1,128)S(1)} %reshape.132), channel_id=1, replica_groups=mesh['nodes'=8,'rep'=4] {'rep'}, dimensions={0}, use_global_device_ids=true | all-gather | bytes 7680 | tf_op jit(solution)/shard_map/all_gather | solution.py:426
  71.2 0.4 convert_reduce_fusion
  71.6 11.3 %all-gather.3.cloned.1.call-done = bf16[1536,512]{1,0:T(8,128)(2,1)} async-done(((bf16[384,512]{1,0:T(8,128)(2,1)}), bf16[1536,512]{1,0:T(8,128)(2,1)}) %all-gather.3.cloned.1.call-update) | async-done | bytes 1572880 | tf_op jit(solution)/shard_map/all_gather | solution.py:447
  82.9 2.5 %fusion.4 = f32[512,512,1]{1,0,2:T(8,128)S(1)} fusion(bf16[1536,512]{1,0:T(8,128)(2,1)} %all-gather.3.cloned.1.call-done, s32[1536]{0:T(1024)S(1)} %reshape.133, f32[512]{0:T(512)S(1)} %broadcast_maximum_fusion), kind=kOutput, calls=%fused_computation.16 | convolution fusion | flops 806354944 | bytes 2629632 | tf_op jit(solution)/shard_map/dot_general | solution.py:449
  85.4 1.8 %convolution_bitcast_fusion.1 = f32[3,512,128]{2,1,0:T(8,128)S(1)} fusion(f32[512,512,1]{1,0,2:T(8,128)S(1)} %fusion.4, f32[3,512,128]{2,1,0:T(8,128)S(1)} %copy-done.8), kind=kOutput, calls=%fused_computation.14 | convolution fusion | flops 1207959552 | bytes 2621440 | tf_op jit(solution)/shard_map/rk,gku->gru/dot_general | solution.py:456
  87.3 0.9 fusion.50
  88.2 0.3 copy-done.1
  88.5 0.2 copy-done.2
  88.8 47.0 %shard_map.185 = bf16[128,512]{1,0:T(8,128)(2,1)S(1)} custom-call(bf16[512,128]{1,0:T(8,128)(2,1)S(1)} %get-tuple-element.4.part_ref, s32[128,1]{1,0:T(8,128)S(1)} %copy.50.src_ref, f32[128,16]{1,0:T(8,128)S(1)} %fusion.43.index_ref, f32[128,16]{1,0:T(8,128)S(1)} %broadcast_subtract_fusion.gap_ref, f32[1,128]{1,0:T(1,128)S(1)} %bitcast.95, ...), custom_call_target="tpu_custom_call" | custom-call | tf_op jit(solution)/shard_map/pallas_call | solution.py:234
  135.8 0.7 copy.56
  (46 shorter events, 0.3 us)
Async XLA Ops:
  7.2 36.6 %copy-start = (bf16[1152,512]{1,0:T(8,128)(2,1)S(1)}, bf16[1152,512]{1,0:T(8,128)(2,1)}, u32[]{:S(2)}) copy-start(bf16[1152,512]{1,0:T(8,128)(2,1)} %param.29) | copy-start | bytes 3538948
  7.2 13.5 %copy-start.6 = (s32[512]{0:T(512)S(1)}, s32[512]{0:T(512)}, u32[]{:S(2)}) copy-start(s32[512]{0:T(512)} %param.19) | copy-start | bytes 6148
  11.5 7.8 %all-to-all-start = ((s32[8,1,32]{2,1,0:T(1,128)}), s32[8,1,32]{2,1,0:T(1,128)S(1)}, u32[]{:S(2)}, u32[]{:S(2)}) async-start(s32[8,1,32]{2,1,0:T(1,128)} %all_to_all.18), calls=%async_computation | async-start | bytes 8192 | tf_op jit(solution)/shard_map/all_to_all | solution.py:424
  20.7 8.9 %copy-start.7 = (f32[512,512]{1,0:T(8,128)S(1)}, f32[512,512]{1,0:T(8,128)}, u32[]{:S(2)}) copy-start(f32[512,512]{1,0:T(8,128)} %param.18) | copy-start | bytes 3145732
  23.3 8.5 %all-to-all-start.2 = ((s32[8,1,32]{2,1,0:T(1,128)}), s32[8,1,32]{2,1,0:T(1,128)S(1)}, u32[]{:S(2)}, u32[]{:S(2)}) async-start(s32[8,1,32]{2,1,0:T(1,128)} %all_to_all.21), calls=%async_computation.2 | async-start | bytes 8192 | tf_op jit(solution)/shard_map/all_to_all | solution.py:430
  31.8 11.1 %all-to-all-start.1 = ((bf16[8,32,512]{2,1,0:T(8,128)(2,1)}), bf16[8,32,512]{2,1,0:T(8,128)(2,1)S(1)}, u32[]{:S(2)}, u32[]{:S(2)}) async-start(bf16[8,32,512]{2,1,0:T(8,128)(2,1)} %bitcast.3), calls=%async_computation.1 | async-start | bytes 524288 | tf_op jit(solution)/shard_map/all_to_all | solution.py:429
  38.1 4.2 %copy-start.14 = (s32[128]{0:T(128)S(1)}, s32[128]{0:T(128)}, u32[]{:S(2)}) copy-start(s32[128]{0:T(128)} %param.23) | copy-start | bytes 1540
  38.1 4.2 %copy-start.4 = (f32[128]{0:T(128)S(1)}, f32[128]{0:T(128)}, u32[]{:S(2)}) copy-start(f32[128]{0:T(128)} %param.28) | copy-start | bytes 1540
  38.1 4.2 %copy-start.5 = (f32[128]{0:T(128)S(1)}, f32[128]{0:T(128)}, u32[]{:S(2)}) copy-start(f32[128]{0:T(128)} %param.27) | copy-start | bytes 1540
  44.3 12.5 %copy-start.9 = (s32[128,16,1]{0,2,1:T(1,128)S(1)}, s32[128,16,1]{0,2,1:T(1,128)}, u32[]{:S(2)}) copy-start(s32[128,16,1]{0,2,1:T(1,128)} %param.24) | copy-start | bytes 24580
  44.4 12.6 %copy-start.10 = (s32[128,16]{0,1:T(8,128)S(1)}, s32[128,16]{0,1:T(8,128)}, u32[]{:S(2)}) copy-start(s32[128,16]{0,1:T(8,128)} %param.25) | copy-start | bytes 24580
  44.4 12.7 %copy-start.11 = (s32[128,16]{0,1:T(8,128)S(1)}, s32[128,16]{0,1:T(8,128)}, u32[]{:S(2)}) copy-start(s32[128,16]{0,1:T(8,128)} %param.26) | copy-start | bytes 24580
  46.1 11.0 %copy-start.12 = (s32[128]{0:T(128)S(1)}, s32[128]{0:T(128)}, u32[]{:S(2)}) copy-start(s32[128]{0:T(128)} %param.20) | copy-start | bytes 1540
  46.1 11.2 %copy-start.13 = (f32[4,128]{1,0:T(4,128)S(1)}, f32[4,128]{1,0:T(4,128)}, u32[]{:S(2)}) copy-start(f32[4,128]{1,0:T(4,128)} %param.32) | copy-start | bytes 6148
  46.1 9.9 %all-to-all-start.3 = ((bf16[8,32,512]{2,1,0:T(8,128)(2,1)}), bf16[8,32,512]{2,1,0:T(8,128)(2,1)S(1)}, u32[]{:S(2)}, u32[]{:S(2)}) async-start(bf16[8,32,512]{2,1,0:T(8,128)(2,1)} %bitcast.5), calls=%async_computation.3 | async-start | bytes 524288 | tf_op jit(solution)/shard_map/all_to_all | solution.py:443
  51.9 31.0 %all-gather.3.cloned.1.call-start = ((), (), s32[]{:S(2)}) async-start(), calls=%async_computation.4 | async-start | bytes 1966080 | tf_op jit(solution)/shard_map/all_gather | solution.py:447
  82.9 2.5 %copy-start.8 = (f32[3,512,128]{2,1,0:T(8,128)S(1)}, f32[3,512,128]{2,1,0:T(8,128)}, u32[]{:S(2)}) copy-start(f32[3,512,128]{2,1,0:T(8,128)} %param.30) | copy-start | bytes 2359300
  87.2 1.3 copy-start.1
  87.3 1.4 %copy-start.2 = (bf16[512,512]{1,0:T(8,128)(2,1)S(1)}, bf16[512,512]{1,0:T(8,128)(2,1)}, u32[]{:S(2)}) copy-start(bf16[512,512]{1,0:T(8,128)(2,1)} %wq_ref.1) | copy-start | bytes 1572868
  87.3 1.5 %copy-start.3 = (bf16[128,1024]{1,0:T(8,128)(2,1)S(1)}, bf16[128,1024]{1,0:T(8,128)(2,1)}, u32[]{:S(2)}) copy-start(bf16[128,1024]{1,0:T(8,128)(2,1)} %wt_ref.1) | copy-start | bytes 786436
Sparse Core Ops, SparseCore 0:
  56.9 25.9 all-gather.2

commit v2 on v1

--- a/solution.py
+++ b/solution.py
@@ -248,6 +248,302 @@
     )(part, src, index, gaps, freq, phase, wq, wkv, wt)
 
 
+def dot_rows(a, b):
+    return lax.dot_general(a, b, (((0,), (0,)), ((), ())), preferred_element_type=F32)
+
+
+def three_pass(a, b_high, b_low):
+    high, low = split(a)
+    return dot32(high, b_high) + dot32(low, b_high) + dot32(high, b_low)
+
+
+def silu(v):
+    return v / (1.0 + jnp.exp(-v))
+
+
+def sigmoid(v):
+    return 1.0 / (1.0 + jnp.exp(-v))
+
+
+def update_kernel(
+    groups,
+    memory_ref,
+    tick_ref,
+    cols_ref,
+    src_ref,
+    freq_ref,
+    phase_ref,
+    wm_ref,
+    wi_ref,
+    wh_ref,
+    bias_ref,
+    out_ref,
+    half_ref,
+    rows_of,
+    ids_out,
+    ids_in,
+    serve,
+    reply,
+    outgoing,
+    messages,
+    names,
+    win_high,
+    win_low,
+    state,
+    send_ids,
+    recv_ids,
+    send_rows,
+    recv_rows,
+    send_msgs,
+    recv_msgs,
+    send_x,
+    recv_x,
+    send_c,
+    recv_c,
+):
+    node = lax.axis_index("nodes")
+    rep = lax.axis_index("rep")
+    x, c = rep // 2, rep % 2
+    rows, width = memory_ref.shape
+    unit = out_ref.shape[1]
+    events = cols_ref.shape[0]
+    cap = reply.shape[0] // groups
+    per = 128 // cap
+    tiles = groups // per
+    across_x = (node, ((x + 1) % 2) * 2 + c)
+    across_c = (node, x * 2 + (c + 1) % 2)
+
+    barrier = pltpu.get_barrier_semaphore()
+    partners = [((node + d) % groups, rep) for d in range(1, groups)] + [across_x, across_c]
+    for device in partners:
+        pl.semaphore_signal(barrier, inc=1, device_id=device, device_id_type=MESH)
+
+    owner = cols_ref[:, 0:1]
+    target = cols_ref[:, 1:2]
+    source = cols_ref[:, 2:3]
+    ticks = cols_ref[:, 3:4]
+    lane = lax.broadcasted_iota(jnp.int32, (events, 128), 1).astype(F32)
+    row_i = lax.broadcasted_iota(jnp.int32, (events, events), 0)
+    col_i = lax.broadcasted_iota(jnp.int32, (events, events), 1)
+    named = owner == lane
+    before = dot32((row_i > col_i).astype(BF16), named.astype(BF16))
+    rank = jnp.sum(jnp.where(named, before, 0.0), axis=1, keepdims=True)
+    slot = owner * cap + rank
+    place_lane = rank + ((node % per) * cap).astype(F32)
+    at_lane = place_lane == lane
+    for g in range(groups):
+        took = jnp.where(at_lane & (owner == float(g)), target + 1.0, 0.0)
+        line = jnp.sum(took, axis=0, keepdims=True) - 1.0
+        ids_out[g] = jnp.broadcast_to(line.astype(jnp.int32), (8, 128))
+    ids_in[node] = ids_out[node]
+
+    def piece_of(ref, n):
+        return ref.at[pl.ds(pl.multiple_of(n * cap, cap), cap), :]
+
+    def send_to(d, src, dst, send, recv):
+        return pltpu.make_async_remote_copy(
+            src_ref=src,
+            dst_ref=dst,
+            send_sem=send.at[d - 1],
+            recv_sem=recv.at[d - 1],
+            device_id=((node + d) % groups, rep),
+            device_id_type=MESH,
+        )
+
+    def ids_copy(d):
+        there = (node + d) % groups
+        return send_to(d, ids_out.at[there], ids_in.at[node], send_ids, recv_ids)
+
+    def rows_copy(d):
+        there = (node + d) % groups
+        return send_to(d, piece_of(serve, there), piece_of(reply, node), send_rows, recv_rows)
+
+    def far_slot():
+        return messages.at[rep, pl.ds(pl.multiple_of(events + node * cap, cap), cap), :]
+
+    def msgs_copy(d):
+        there = (node + d) % groups
+        return send_to(d, piece_of(outgoing, there), far_slot(), send_msgs, recv_msgs)
+
+    def part_of(r, p):
+        if p == tiles + 1:
+            return names.at[r]
+        return messages.at[r, p * 128 : (p + 1) * 128, :]
+
+    def over_x(p):
+        return pltpu.make_async_remote_copy(
+            src_ref=part_of(rep, p),
+            dst_ref=part_of(rep, p),
+            send_sem=send_x.at[p],
+            recv_sem=recv_x.at[p],
+            device_id=across_x,
+            device_id_type=MESH,
+        )
+
+    def over_c(p, b):
+        r = ((x + b) % 2) * 2 + c
+        return pltpu.make_async_remote_copy(
+            src_ref=part_of(r, p),
+            dst_ref=part_of(r, p),
+            send_sem=send_c.at[p, b],
+            recv_sem=recv_c.at[p, b],
+            device_id=across_c,
+            device_id_type=MESH,
+        )
+
+    started = []
+
+    def start(one):
+        one.start()
+        started.append(one)
+
+    pl.semaphore_wait(barrier, len(partners))
+    for d in range(1, groups):
+        start(ids_copy(d))
+
+    rows_of[:, :width] = memory_ref[...].astype(BF16)
+    old = jnp.broadcast_to(tick_ref[...], (rows, 128))
+    big = jnp.floor(old * (1.0 / 256.0))
+    lanes_r = lax.broadcasted_iota(jnp.int32, (rows, 128), 1)
+    packed = jnp.where(lanes_r == 0, big, jnp.where(lanes_r == 1, old - big * 256.0, 0.0))
+    rows_of[:, width:] = packed.astype(BF16)
+
+    def encoded(found):
+        last = found[:, width : width + 1] * 256.0 + found[:, width + 1 : width + 2]
+        return jnp.cos((ticks - last) * freq_ref[...] + phase_ref[...]).astype(BF16)
+
+    for d in range(1, groups):
+        ids_copy(d).wait_recv()
+    row_id = lax.broadcasted_iota(jnp.int32, (rows, 128), 0)
+    lines = [src_ref[...]]
+    for h in range(tiles):
+        line = ids_in[h * per][0:1, :]
+        for q in range(1, per):
+            line = jnp.maximum(line, ids_in[h * per + q][0:1, :])
+        lines.append(line)
+        wanted = (row_id == line).astype(BF16)
+        serve[h * 128 : (h + 1) * 128, :] = dot_rows(wanted, rows_of[...]).astype(BF16)
+    for d in range(1, groups):
+        start(rows_copy(d))
+    here = pl.ds(pl.multiple_of(node * cap, cap), cap)
+    reply[here, :] = serve[here, :]
+    blank = jnp.full((8 - len(lines), 128), -1, jnp.int32)
+    names[rep] = jnp.concatenate(lines + [blank], axis=0)
+    start(over_x(tiles + 1))
+    start(over_c(tiles + 1, 0))
+
+    near = (source == lax.broadcasted_iota(jnp.int32, (events, rows), 1).astype(F32)).astype(BF16)
+    near = dot32(near, rows_of[...])
+    near_rows = near[:, :width].astype(BF16)
+    w_first = wm_ref[0:width, :]
+    w_second = wm_ref[width : 2 * width, :]
+    w_time = wm_ref[2 * width :, :]
+    src_sum = dot32(near_rows, w_first) + dot32(encoded(near), w_time)
+    dst_sum = dot32(near_rows, w_second)
+    chosen = (slot == lax.broadcasted_iota(jnp.int32, (events, groups * cap), 1).astype(F32)).astype(
+        BF16
+    )
+
+    for d in range(1, groups):
+        rows_copy(d).wait_recv()
+    far = dot32(chosen, reply[...])
+    far_rows = far[:, :width].astype(BF16)
+    msg_dst = silu(dst_sum + dot32(far_rows, w_first) + dot32(encoded(far), w_time)).astype(BF16)
+    outgoing[...] = dot_rows(chosen, msg_dst).astype(BF16)
+    for d in range(1, groups):
+        start(msgs_copy(d))
+    messages[rep, 0:events, :] = silu(src_sum + dot32(far_rows, w_second)).astype(BF16)
+    start(over_x(0))
+    start(over_c(0, 0))
+    messages[rep, pl.ds(pl.multiple_of(events + node * cap, cap), cap), :] = outgoing[here, :]
+
+    over_x(tiles + 1).wait_recv()
+    start(over_c(tiles + 1, 1))
+    mem_high, mem_low = split(memory_ref[...])
+    for g in range(3):
+        place_g = slice(g * unit, (g + 1) * unit)
+        high, low = split(wi_ref[g])
+        win_high[:, place_g] = high
+        win_low[:, place_g] = low
+        high, low = split(wh_ref[g])
+        state[:, place_g] = dot32(mem_high, high) + dot32(mem_low, high) + dot32(mem_high, low)
+
+    for d in range(1, groups):
+        msgs_copy(d).wait_recv()
+    for p in range(1, tiles + 1):
+        start(over_x(p))
+        start(over_c(p, 0))
+    for p in range(tiles + 1):
+        over_x(p).wait_recv()
+        start(over_c(p, 1))
+    for p in range(tiles + 2):
+        over_c(p, 0).wait_recv()
+    for p in range(tiles + 2):
+        over_c(p, 1).wait_recv()
+
+    sums = jnp.zeros((rows, messages.shape[2]), F32)
+    hits = jnp.zeros((rows, 128), F32)
+    for r in range(4):
+        tile = names[r]
+        parts = [(row_id == tile[p : p + 1, :]).astype(F32) for p in range(tiles + 1)]
+        for part in parts:
+            hits += part
+        sums += dot32(jnp.concatenate(parts, axis=1).astype(BF16), messages[r])
+    counts = jnp.sum(hits, axis=1, keepdims=True)
+    mean = sums / jnp.maximum(counts, 1.0)
+    fed = three_pass(mean, win_high[...], win_low[...])
+    was = memory_ref[:, pl.ds(pl.multiple_of(rep * unit, unit), unit)]
+    update = sigmoid(fed[:, :unit] + state[:, :unit] + bias_ref[0:1, :])
+    reset = sigmoid(fed[:, unit : 2 * unit] + state[:, unit : 2 * unit] + bias_ref[1:2, :])
+    cand = jnp.tanh(
+        fed[:, 2 * unit :] + bias_ref[2:3, :] + reset * (state[:, 2 * unit :] + bias_ref[3:4, :])
+    )
+    fresh = (1.0 - update) * cand + update * was
+    fresh = jnp.where(counts > 0.0, fresh, was)
+    out_ref[...] = fresh
+    half_ref[...] = fresh.astype(BF16)
+    for one in started:
+        one.wait_send()
+
+
+def update_rows(memory, tick, cols, src, freq, phase, wm, wi, wh, bias, groups):
+    rows, width = memory.shape
+    unit = bias.shape[1]
+    events = cols.shape[0]
+    cap = 2 * events // groups
+    slots = groups * cap
+    pieces = events // 128 + slots // 128
+    msg = wm.shape[1]
+    dma = pltpu.SemaphoreType.DMA
+    counts = [(groups - 1,)] * 3 + [(pieces + 1,), (pieces + 1, 2)]
+    return pl.pallas_call(
+        functools.partial(update_kernel, groups),
+        out_shape=(
+            jax.ShapeDtypeStruct((rows, unit), F32),
+            jax.ShapeDtypeStruct((rows, unit), BF16),
+        ),
+        in_specs=[pl.BlockSpec(memory_space=pltpu.VMEM)] * 10,
+        out_specs=(pl.BlockSpec(memory_space=pltpu.VMEM),) * 2,
+        scratch_shapes=[
+            pltpu.VMEM((rows, width + 128), BF16),
+            pltpu.VMEM((groups, 8, 128), jnp.int32),
+            pltpu.VMEM((groups, 8, 128), jnp.int32),
+            pltpu.VMEM((slots, width + 128), BF16),
+            pltpu.VMEM((slots, width + 128), BF16),
+            pltpu.VMEM((slots, msg), BF16),
+            pltpu.VMEM((4, events + slots, msg), BF16),
+            pltpu.VMEM((4, 8, 128), jnp.int32),
+            pltpu.VMEM((msg, 3 * unit), BF16),
+            pltpu.VMEM((msg, 3 * unit), BF16),
+            pltpu.VMEM((rows, 3 * unit), F32),
+        ]
+        + [dma(shape) for shape in counts for _ in range(2)],
+        compiler_params=pltpu.CompilerParams(
+            collective_id=0, has_side_effects=True, vmem_limit_bytes=40 * 1024 * 1024
+        ),
+    )(memory, tick, cols, src, freq, phase, wm, wi, wh, bias)
+
+
 def encode(gaps, freq, phase):
     return jnp.cos(gaps[..., None] * freq + phase)
 
@@ -405,65 +701,28 @@
     w_keyval_time,
 ):
     groups = lax.axis_size("nodes")
-    events = src_local.shape[0]
     rows_here = memory.shape[0]
-    width_m = memory.shape[1]
-    msg_width = w_message.shape[1]
-    dst_cap = max(2, 2 * events // groups)
-    dst_slot = place(dst_owner[:, 0], groups, dst_cap)
-    dst_ids = (
-        jnp.full((groups * dst_cap,), -1, jnp.int32)
-        .at[dst_slot]
-        .set(dst_local)
-        .reshape(groups, dst_cap)
-    )
-    mem_half = memory.astype(jnp.bfloat16)
-    near_rows = mem_half[src_local]
-    near_ticks = last_tick[src_local]
     ticks = event_tick.astype(jnp.float32)
-    got_dst = lax.all_to_all(dst_ids, "nodes", split_axis=0, concat_axis=0, tiled=True)
-    names = jnp.concatenate([src_local, got_dst.reshape(-1)])
-    names = lax.all_gather(names, "rep", axis=0, tiled=True)
-    safe_dst = jnp.maximum(got_dst, 0)
-    reply_rows, reply_ticks = (
-        lax.all_to_all(mem_half[safe_dst], "nodes", split_axis=0, concat_axis=0, tiled=True),
-        lax.all_to_all(last_tick[safe_dst], "nodes", split_axis=0, concat_axis=0, tiled=True),
-    )
-    far_rows = reply_rows.reshape(-1, width_m)[dst_slot]
-    far_ticks = reply_ticks.reshape(-1)[dst_slot]
-    src_time = encode(ticks - near_ticks.astype(jnp.float32), freq, phase).astype(jnp.bfloat16)
-    dst_time = encode(ticks - far_ticks.astype(jnp.float32), freq, phase).astype(jnp.bfloat16)
-    msg_src, msg_dst = message_pair(near_rows, far_rows, src_time, dst_time, w_message)
-    outgoing = (
-        jnp.zeros((groups * dst_cap, msg_width), jnp.bfloat16)
-        .at[dst_slot]
-        .set(msg_dst)
-        .reshape(groups, dst_cap, msg_width)
-    )
-    incoming = lax.all_to_all(outgoing, "nodes", split_axis=0, concat_axis=0, tiled=True)
-    far_msgs = incoming.reshape(-1, msg_width)
-    row_ids = jnp.arange(rows_here, dtype=jnp.int32)[:, None]
-    messages = jnp.concatenate([msg_src, far_msgs], axis=0)
-    messages = lax.all_gather(messages, "rep", axis=0, tiled=True)
-    hits = (row_ids == names[None, :]).astype(jnp.bfloat16)
-    sums = jnp.dot(hits, messages, preferred_element_type=jnp.float32)
-    counts = jnp.sum(hits.astype(jnp.float32), axis=1)
-    unit_width = gru_bias.shape[1]
-    start = lax.axis_index("rep") * unit_width
-    state_part = lax.dynamic_slice_in_dim(memory, start, unit_width, 1)
-    mean = sums / jnp.maximum(counts, 1.0)[:, None]
-    highest = lax.Precision.HIGHEST
-    a_parts = jnp.einsum("rk,gku->gru", mean, gru_input, precision=highest)
-    b_parts = jnp.einsum("rk,gku->gru", memory, gru_hidden, precision=highest)
-    update = jax.nn.sigmoid(a_parts[0] + b_parts[0] + gru_bias[0])
-    reset = jax.nn.sigmoid(a_parts[1] + b_parts[1] + gru_bias[1])
-    cand = jnp.tanh(a_parts[2] + gru_bias[2] + reset * (b_parts[2] + gru_bias[3]))
-    fresh = (1.0 - update) * cand + update * state_part
-    new_part = jnp.where((counts > 0.0)[:, None], fresh, state_part)
+    cols = jnp.stack(
+        [dst_owner[:, 0].astype(F32), dst_local.astype(F32), src_local.astype(F32), ticks], axis=1
+    )
+    new_part, new_half = update_rows(
+        memory,
+        last_tick.astype(F32)[:, None],
+        cols,
+        src_local[None, :],
+        freq[None, :],
+        phase[None, :],
+        w_message,
+        gru_input,
+        gru_hidden,
+        gru_bias,
+        groups,
+    )
     index = (nbr_owner[:, :, 0] * rows_here + nbr_local).astype(jnp.float32)
     gaps = ticks[:, None] - nbr_tick.astype(jnp.float32)
     embed = attend(
-        new_part.astype(jnp.bfloat16),
+        new_half,
         src_local[:, None],
         index,
         gaps,

time: 144 us -> 91.7 us (0.64)
  Pallas kernels: 47 us -> 78.2 us
  starting transfers between devices: 23.9 us -> 0 us
  waiting for transfers between devices: 17.3 us -> 0 us
  between operations: 14.4 us -> 0.8 us
  blocking collectives: 10.7 us -> 0 us
  matrix products: 7.83 us -> 0 us
  local copies, waits for them, and re-layouts: 14.8 us -> 9.48 us
  other arithmetic: 7.46 us -> 2.78 us
    pallas_call x0 -> x1, Pallas kernels: none -> 31.8 us  [update_rows(): pl.pallas_call(functools.partial(update_kernel, groups), out_shape=(jax.S...]
    all_to_all x4 -> x0, starting transfers between devices: 23.9 us -> none  [the longest x1 6.35 us: on_device(): lax.all_to_all(mem_half[safe_dst], 'nodes', split_axis=0, concat_axis=0,...]
    all_gather x1 -> x0, waiting for transfers between devices: 11.3 us -> none  [on_device(): messages = lax.all_gather(messages, 'rep', axis=0, tiled=True)]
    all_gather x1 -> x0, blocking collectives: 10.7 us -> none  [on_device(): names = lax.all_gather(names, 'rep', axis=0, tiled=True)]
    gather x6 -> x0, local copies, waits for them, and re-layouts: 8.03 us -> none  [the longest x1 1.95 us: on_device(): last_tick[safe_dst]]
    dot_general x4 -> x0, matrix products: 7.83 us -> none  [the longest x1 2.97 us: on_device(): b_parts = jnp.einsum('rk,gku->gru', memory, gru_hidden, precision=highest)]
    unnamed x35 -> x38, local copies, waits for them, and re-layouts: 1.48 us -> 9.01 us
    all_to_all x4 -> x0, waiting for transfers between devices: 5.97 us -> none  [the longest x1 4.07 us: on_device(): lax.all_to_all(outgoing, 'nodes', split_axis=0, concat_axis=0, tiled=True)]
  transfers between devices with their start and end apart: 5 -> 0, of which waited for: 4 -> 0; matrix products, arithmetic and copies ran while one was open for 8% -> 0% of each run, Pallas kernels for 0% -> 0%
where the time goes in v2:
time: 91.7 us; the launch traced here: 91.3 us
  Pallas kernels  78.2 us (85%)
  local copies, waits for them, and re-layouts  9.48 us (10%)
  other arithmetic  2.78 us (3%)
    pallas_call x1, Pallas kernels, attend(): pl.pallas_call(functools.partial(attend_kernel, groups), out_shape=jax.Sh...  46.4 us
    pallas_call x1, Pallas kernels, update_rows(): pl.pallas_call(functools.partial(update_kernel, groups), out_shape=(jax.S...  31.8 us
    unnamed x38, local copies, waits for them, and re-layouts  9.01 us

profile of v2, /device:TPU:25, one launch (start us, length us, event | category | flops | bytes accessed | tf_op | source)
XLA Modules:
  0.0 91.3 jit_solution(13019549436978611864)
XLA Ops:
  0.6 0.7 fusion.1
  1.3 0.7 convert_bitcast_fusion
  2.0 0.7 convert_element_type.23
  2.6 0.1 copy.44.cols_ref
  2.7 0.7 convert_element_type.22
  3.4 0.1 copy.43.tick_ref
  3.6 0.0 copy-start
  3.6 1.3 %copy-done = bf16[1152,512]{1,0:T(8,128)(2,1)S(1)} copy-done((bf16[1152,512]{1,0:T(8,128)(2,1)S(1)}, bf16[1152,512]{1,0:T(8,128)(2,1)}, u32[]{:S(2)}) %copy-start) | copy-done | bytes 1179672
  4.9 0.0 copy-start.1
  4.9 1.2 %copy-done.1 = f32[512,512]{1,0:T(8,128)S(1)} copy-done((f32[512,512]{1,0:T(8,128)S(1)}, f32[512,512]{1,0:T(8,128)}, u32[]{:S(2)}) %copy-start.1) | copy-done | bytes 1048600
  6.1 0.0 copy-start.3
  6.1 1.1 %copy-done.3 = f32[3,512,128]{2,1,0:T(8,128)S(1)} copy-done((f32[3,512,128]{2,1,0:T(8,128)S(1)}, f32[3,512,128]{2,1,0:T(8,128)}, u32[]{:S(2)}) %copy-start.3) | copy-done | bytes 786456
  7.2 0.0 copy-start.4
  7.2 1.1 %copy-done.4 = f32[3,512,128]{2,1,0:T(8,128)S(1)} copy-done((f32[3,512,128]{2,1,0:T(8,128)S(1)}, f32[3,512,128]{2,1,0:T(8,128)}, u32[]{:S(2)}) %copy-start.4) | copy-done | bytes 786456
  8.4 0.0 copy-start.7
  8.4 0.7 copy-done.7
  9.0 0.0 copy-start.9
  9.0 0.7 copy-done.9
  9.7 0.0 copy-start.10
  9.7 0.7 copy-done.10
  10.3 0.0 copy-start.12
  10.4 0.7 copy-done.12
  11.0 0.0 copy-start.16
  11.0 0.0 copy-start.14
  11.0 0.0 copy-start.15
  11.0 0.0 copy-start.2
  11.0 0.0 copy-start.5
  11.0 0.0 copy-start.6
  11.1 0.0 copy-start.11
  11.1 0.0 copy-start.13
  11.1 31.8 %shard_map.185 = (f32[512,128]{1,0:T(8,128)S(1)}, bf16[512,128]{1,0:T(8,128)(2,1)S(1)}) custom-call(f32[512,512]{1,0:T(8,128)S(1)} %copy-done.1, f32[512,1]{1,0:T(8,128)S(1)} %copy.43.tick_ref, f32[128,4]{1,0:T(8,128)S(1)} %copy.44.cols_ref, s32[1,128]{1,0:T(1,128)S(1)} %bitcast.15, f32[1,128]{1,0:T(1,128)S(1)} %bitcast.17, f32[1,128]{1,0:T(1,128)S(1)} %bitcast.19, ...), custom_call_target="tpu_custom_call" | custom-call | tf_op jit(solution)/shard_map/pallas_call | solution.py:519
  42.9 0.0 copy-done.16
  42.9 0.1 copy.48
  43.0 0.1 broadcast_subtract_fusion.gap_ref
  43.1 0.0 copy-done.14
  43.1 0.1 copy.45
  43.2 0.0 copy-done.15
  43.2 0.1 copy.46
  43.3 0.0 copy-done.8
  43.3 0.1 copy.49.src_ref
  43.4 0.0 copy-done.2
  43.4 0.0 copy-done.5
  43.4 0.0 copy-done.6
  43.4 0.0 copy-done.11
  43.5 0.0 copy-done.13
  43.5 46.4 %shard_map.186 = bf16[128,512]{1,0:T(8,128)(2,1)S(1)} custom-call(bf16[512,128]{1,0:T(8,128)(2,1)S(1)} %get-tuple-element.5.part_ref, s32[128,1]{1,0:T(8,128)S(1)} %copy.49.src_ref, f32[128,16]{1,0:T(8,128)S(1)} %fusion.index_ref, f32[128,16]{1,0:T(8,128)S(1)} %broadcast_subtract_fusion.gap_ref, f32[1,128]{1,0:T(1,128)S(1)} %bitcast.18, ...), custom_call_target="tpu_custom_call" | custom-call | tf_op jit(solution)/shard_map/pallas_call | solution.py:234
  89.9 0.7 copy.53
  90.6 0.7 copy.54
  (4 shorter events, 0.0 us)
Async XLA Ops:
  3.6 1.3 %copy-start = (bf16[1152,512]{1,0:T(8,128)(2,1)S(1)}, bf16[1152,512]{1,0:T(8,128)(2,1)}, u32[]{:S(2)}) copy-start(bf16[1152,512]{1,0:T(8,128)(2,1)} %wm_ref.1) | copy-start | bytes 3538948
  4.9 1.2 %copy-start.1 = (f32[512,512]{1,0:T(8,128)S(1)}, f32[512,512]{1,0:T(8,128)}, u32[]{:S(2)}) copy-start(f32[512,512]{1,0:T(8,128)} %memory_ref.1) | copy-start | bytes 3145732
  6.1 1.1 %copy-start.3 = (f32[3,512,128]{2,1,0:T(8,128)S(1)}, f32[3,512,128]{2,1,0:T(8,128)}, u32[]{:S(2)}) copy-start(f32[3,512,128]{2,1,0:T(8,128)} %wi_ref.1) | copy-start | bytes 2359300
  7.2 1.1 %copy-start.4 = (f32[3,512,128]{2,1,0:T(8,128)S(1)}, f32[3,512,128]{2,1,0:T(8,128)}, u32[]{:S(2)}) copy-start(f32[3,512,128]{2,1,0:T(8,128)} %wh_ref.1) | copy-start | bytes 2359300
  8.4 0.7 copy-start.7
  9.0 0.7 copy-start.9
  9.7 0.7 copy-start.10
  10.3 0.7 copy-start.12
  11.0 31.9 %copy-start.16 = (s32[128,16]{0,1:T(8,128)S(1)}, s32[128,16]{0,1:T(8,128)}, u32[]{:S(2)}) copy-start(s32[128,16]{0,1:T(8,128)} %param.26) | copy-start | bytes 24580
  11.0 32.1 %copy-start.14 = (s32[128,16,1]{0,2,1:T(1,128)S(1)}, s32[128,16,1]{0,2,1:T(1,128)}, u32[]{:S(2)}) copy-start(s32[128,16,1]{0,2,1:T(1,128)} %param.24) | copy-start | bytes 24580
  11.0 32.2 %copy-start.15 = (s32[128,16]{0,1:T(8,128)S(1)}, s32[128,16]{0,1:T(8,128)}, u32[]{:S(2)}) copy-start(s32[128,16]{0,1:T(8,128)} %param.25) | copy-start | bytes 24580
  11.0 32.3 %copy-start.8 = (s32[128]{0:T(128)S(1)}, s32[128]{0:T(128)}, u32[]{:S(2)}) copy-start(s32[128]{0:T(128)} %param.20) | copy-start | bytes 1540
  11.0 32.4 %copy-start.2 = (bf16[512,1024]{1,0:T(8,128)(2,1)S(1)}, bf16[512,1024]{1,0:T(8,128)(2,1)}, u32[]{:S(2)}) copy-start(bf16[512,1024]{1,0:T(8,128)(2,1)} %wkv_ref.1) | copy-start | bytes 3145732
  11.0 32.4 %copy-start.5 = (bf16[512,512]{1,0:T(8,128)(2,1)S(1)}, bf16[512,512]{1,0:T(8,128)(2,1)}, u32[]{:S(2)}) copy-start(bf16[512,512]{1,0:T(8,128)(2,1)} %wq_ref.1) | copy-start | bytes 1572868
  11.0 32.4 %copy-start.6 = (bf16[128,1024]{1,0:T(8,128)(2,1)S(1)}, bf16[128,1024]{1,0:T(8,128)(2,1)}, u32[]{:S(2)}) copy-start(bf16[128,1024]{1,0:T(8,128)(2,1)} %wt_ref.1) | copy-start | bytes 786436
  11.1 32.4 %copy-start.11 = (f32[128]{0:T(128)S(1)}, f32[128]{0:T(128)}, u32[]{:S(2)}) copy-start(f32[128]{0:T(128)} %param.27) | copy-start | bytes 1540
  11.1 32.4 %copy-start.13 = (f32[128]{0:T(128)S(1)}, f32[128]{0:T(128)}, u32[]{:S(2)}) copy-start(f32[128]{0:T(128)} %param.28) | copy-start | bytes 1540

commit v3 on v2

--- a/solution.py
+++ b/solution.py
@@ -41,11 +41,16 @@
     gap_ref,
     freq_ref,
     phase_ref,
+    wq_hbm,
+    wkv_hbm,
+    wt_hbm,
+    out_ref,
     wq_ref,
     wkv_ref,
     wt_ref,
-    out_ref,
+    load_sem,
     table,
+    found,
     keyval,
     scores,
     send_z,
@@ -57,6 +62,10 @@
     send_c,
     recv_c,
 ):
+    pairs = [(wt_hbm, wt_ref), (wq_hbm, wq_ref), (wkv_hbm, wkv_ref)]
+    loads = [pltpu.make_async_copy(a, b, load_sem.at[i]) for i, (a, b) in enumerate(pairs)]
+    for load in loads:
+        load.start()
     node = lax.axis_index("nodes")
     rep = lax.axis_index("rep")
     deep = groups // 2
@@ -143,6 +152,8 @@
         start(first(h, 0))
         start(second(h, 0, 0))
         start(core(h, 0, 0, 0))
+    for load in loads:
+        load.wait()
     time_part(0)
     for d in range(1, deep):
         for h in range(2):
@@ -154,31 +165,57 @@
             time_part(d)
     for g in range(deep, steps):
         time_part(g)
-    for d in range(deep):
+
+    size = batch * events
+    lanes = lax.broadcasted_iota(jnp.int32, (size, rows), 1)
+
+    def forward_first(d):
         for h in range(2):
             first(h, d).wait_recv()
             start(second(h, d, 1))
             start(core(h, d, 1, 0))
-    for d in range(deep):
+
+    def forward_second(d):
         for k in range(2):
             for h in range(2):
                 second(h, d, k).wait_recv()
                 start(core(h, d, k, 1))
-    for d in range(deep):
+
+    def look_up(d):
         for k in range(2):
             for b in range(2):
                 for h in range(2):
                     core(h, d, k, b).wait_recv()
-    for one in started:
-        one.wait_send()
-
+
+        @pl.loop(0, steps)
+        def _(g):
+            names = column(index_ref, g * batch, batch).astype(jnp.int32)
+            here = pl.ds(pl.multiple_of(g * size, size), size)
+            total = jnp.zeros((size, width), F32)
+            for k in range(2):
+                n, _ = where_of(0, d, k, 0)
+                chosen = (names - n * rows == lanes).astype(BF16)
+                total += dot32(chosen, table[pl.ds(pl.multiple_of(n * rows, rows), rows), :])
+            if d > 0:
+                total += found[here, :].astype(F32)
+            found[here, :] = total.astype(BF16)
+
+    forward_first(0)
+    forward_second(0)
+    for d in range(1, deep):
+        forward_first(d)
+        look_up(d - 1)
+        forward_second(d)
     lane_row = lax.broadcasted_iota(jnp.int32, (events, rows), 1)
     hit = (src_ref[...] == lane_row).astype(BF16)
     mine = dot32(hit, table[block_rows, :]).astype(BF16)
     query = dot32(mine, wq_ref[...]).astype(BF16).astype(F32) * (1.0 / math.sqrt(HEAD_DIM))
     query = jnp.concatenate([query] * batch, axis=0)
+    look_up(deep - 1)
+    for one in started:
+        one.wait_send()
+
     att = HEADS * HEAD_DIM
-    size = batch * events
     head_sum = (
         lax.broadcasted_iota(jnp.int32, (att, 128), 0) // HEAD_DIM
         == lax.broadcasted_iota(jnp.int32, (att, 128), 1)
@@ -187,17 +224,11 @@
         lax.broadcasted_iota(jnp.int32, (128, att), 1) // HEAD_DIM
         == lax.broadcasted_iota(jnp.int32, (128, att), 0)
     ).astype(BF16)
-    lanes = lax.broadcasted_iota(jnp.int32, (size, rows), 1)
 
     @pl.loop(0, steps)
     def _(g):
-        names = column(index_ref, g * batch, batch).astype(jnp.int32)
         here = pl.ds(pl.multiple_of(g * size, size), size)
-        found = jnp.zeros((size, width), F32)
-        for n in range(groups):
-            chosen = (names == lanes + n * rows).astype(BF16)
-            found += dot32(chosen, table[n * rows : (n + 1) * rows, :])
-        kv = dot32(found.astype(BF16), wkv_ref[...]).astype(BF16).astype(F32)
+        kv = dot32(found[here, :], wkv_ref[...]).astype(BF16).astype(F32)
         kv = kv + keyval[here, :]
         keyval[here, att:] = kv[:, att:]
         high, low = split(query * kv[:, :att])
@@ -234,16 +265,21 @@
     return pl.pallas_call(
         functools.partial(attend_kernel, groups),
         out_shape=jax.ShapeDtypeStruct((events, HEADS * HEAD_DIM), BF16),
-        in_specs=[pl.BlockSpec(memory_space=pltpu.VMEM)] * 9,
+        in_specs=[
+            pl.BlockSpec(memory_space=pltpu.HBM if i > 5 else pltpu.VMEM) for i in range(9)
+        ],
         out_specs=pl.BlockSpec(memory_space=pltpu.VMEM),
-        scratch_shapes=[
+        scratch_shapes=[pltpu.VMEM(v.shape, v.dtype) for v in (wq, wkv, wt)]
+        + [
+            dma((3,)),
             pltpu.VMEM((total, reps * unit), BF16),
+            pltpu.VMEM((events * neighbours, reps * unit), BF16),
             pltpu.VMEM((events * neighbours, wkv.shape[1]), F32),
             pltpu.VMEM((events * neighbours, 128), F32),
         ]
         + sems,
         compiler_params=pltpu.CompilerParams(
-            collective_id=1, has_side_effects=True, vmem_limit_bytes=50 * 1024 * 1024
+            collective_id=1, has_side_effects=True, vmem_limit_bytes=62 * 1024 * 1024
         ),
     )(part, src, index, gaps, freq, phase, wq, wkv, wt)
 
@@ -267,18 +303,23 @@
 
 def update_kernel(
     groups,
-    memory_ref,
+    memory_hbm,
     tick_ref,
     cols_ref,
     src_ref,
     freq_ref,
     phase_ref,
+    wm_hbm,
+    wi_hbm,
+    wh_hbm,
+    bias_ref,
+    out_ref,
+    half_ref,
+    memory_ref,
     wm_ref,
     wi_ref,
     wh_ref,
-    bias_ref,
-    out_ref,
-    half_ref,
+    load_sem,
     rows_of,
     ids_out,
     ids_in,
@@ -313,6 +354,11 @@
     across_x = (node, ((x + 1) % 2) * 2 + c)
     across_c = (node, x * 2 + (c + 1) % 2)
 
+    pairs = [(memory_hbm, memory_ref), (wm_hbm, wm_ref), (wh_hbm, wh_ref), (wi_hbm, wi_ref)]
+    loads = [pltpu.make_async_copy(a, b, load_sem.at[i]) for i, (a, b) in enumerate(pairs)]
+    for load in loads:
+        load.start()
+
     barrier = pltpu.get_barrier_semaphore()
     partners = [((node + d) % groups, rep) for d in range(1, groups)] + [across_x, across_c]
     for device in partners:
@@ -401,6 +447,7 @@
     for d in range(1, groups):
         start(ids_copy(d))
 
+    loads[0].wait()
     rows_of[:, :width] = memory_ref[...].astype(BF16)
     old = jnp.broadcast_to(tick_ref[...], (rows, 128))
     big = jnp.floor(old * (1.0 / 256.0))
@@ -435,6 +482,7 @@
     near = (source == lax.broadcasted_iota(jnp.int32, (events, rows), 1).astype(F32)).astype(BF16)
     near = dot32(near, rows_of[...])
     near_rows = near[:, :width].astype(BF16)
+    loads[1].wait()
     w_first = wm_ref[0:width, :]
     w_second = wm_ref[width : 2 * width, :]
     w_time = wm_ref[2 * width :, :]
@@ -459,6 +507,8 @@
 
     over_x(tiles + 1).wait_recv()
     start(over_c(tiles + 1, 1))
+    loads[2].wait()
+    loads[3].wait()
     mem_high, mem_low = split(memory_ref[...])
     for g in range(3):
         place_g = slice(g * unit, (g + 1) * unit)
@@ -522,9 +572,14 @@
             jax.ShapeDtypeStruct((rows, unit), F32),
             jax.ShapeDtypeStruct((rows, unit), BF16),
         ),
-        in_specs=[pl.BlockSpec(memory_space=pltpu.VMEM)] * 10,
+        in_specs=[
+            pl.BlockSpec(memory_space=pltpu.HBM if i in (0, 6, 7, 8) else pltpu.VMEM)
+            for i in range(10)
+        ],
         out_specs=(pl.BlockSpec(memory_space=pltpu.VMEM),) * 2,
-        scratch_shapes=[
+        scratch_shapes=[pltpu.VMEM(v.shape, v.dtype) for v in (memory, wm, wi, wh)]
+        + [
+            dma((4,)),
             pltpu.VMEM((rows, width + 128), BF16),
             pltpu.VMEM((groups, 8, 128), jnp.int32),
             pltpu.VMEM((groups, 8, 128), jnp.int32),
@@ -539,7 +594,7 @@
         ]
         + [dma(shape) for shape in counts for _ in range(2)],
         compiler_params=pltpu.CompilerParams(
-            collective_id=0, has_side_effects=True, vmem_limit_bytes=40 * 1024 * 1024
+            collective_id=0, has_side_effects=True, vmem_limit_bytes=62 * 1024 * 1024
         ),
     )(memory, tick, cols, src, freq, phase, wm, wi, wh, bias)
 

time: 91.7 us -> 95.6 us (1.043)
  Pallas kernels: 78.2 us -> 85.7 us
  local copies, waits for them, and re-layouts: 9.48 us -> 4.94 us
  other arithmetic: 2.78 us -> 4.03 us
    unnamed x38 -> x14, local copies, waits for them, and re-layouts: 9.01 us -> 2.49 us
    pallas_call x1, Pallas kernels: 46.4 us -> 52.1 us  [attend(): pl.pallas_call(functools.partial(attend_kernel, groups), out_shape=jax.Sh...]
    pallas_call x1, Pallas kernels: 31.8 us -> 33.6 us  [update_rows(): pl.pallas_call(functools.partial(update_kernel, groups), out_shape=(jax.S...]
where the time goes in v3:
time: 95.6 us; the launch traced here: 95.4 us
  Pallas kernels  85.7 us (90%)
  local copies, waits for them, and re-layouts  4.94 us (5%)
  other arithmetic  4.03 us (4%)
    pallas_call x1, Pallas kernels, attend(): pl.pallas_call(functools.partial(attend_kernel, groups), out_shape=jax.Sh...  52.1 us
    pallas_call x1, Pallas kernels, update_rows(): pl.pallas_call(functools.partial(update_kernel, groups), out_shape=(jax.S...  33.6 us
    unnamed x14, local copies, waits for them, and re-layouts  2.49 us

profile of v3, /device:TPU:25, one launch (start us, length us, event | category | flops | bytes accessed | tf_op | source)
XLA Modules:
  0.0 95.4 jit_solution(9000407661373921029)
XLA Ops:
  0.6 0.7 fusion.1
  1.3 0.7 convert_bitcast_fusion
  2.0 0.7 convert_element_type.23
  2.6 0.7 copy.44.cols_ref
  3.4 0.7 convert_element_type.22
  4.1 0.9 copy.43.tick_ref
  4.9 0.0 copy-start.3
  4.9 0.0 copy-start.1
  4.9 0.0 copy-start.2
  4.9 0.0 copy-start.4
  4.9 33.6 %shard_map.185 = (f32[512,128]{1,0:T(8,128)}, bf16[512,128]{1,0:T(8,128)(2,1)}) custom-call(f32[512,512]{1,0:T(8,128)} %memory_hbm.1, f32[512,1]{1,0:T(8,128)} %copy.43.tick_ref, f32[128,4]{1,0:T(8,128)} %copy.44.cols_ref, s32[1,128]{1,0:T(1,128)} %bitcast.16, f32[1,128]{1,0:T(1,128)} %bitcast.18, f32[1,128]{1,0:T(1,128)} %bitcast.20, ...), custom_call_target="tpu_custom_call" | custom-call | tf_op jit(solution)/shard_map/pallas_call | solution.py:569
  38.5 0.0 copy-done.3
  38.5 0.1 copy.48
  38.6 0.7 broadcast_subtract_fusion.gap_ref
  39.3 0.0 copy-done.1
  39.3 0.1 copy.45
  39.4 0.0 copy-done.2
  39.4 0.1 copy.46
  39.5 0.6 fusion.index_ref
  40.2 0.0 copy-done.4
  40.2 0.0 copy-start
  40.2 0.7 copy.49.src_ref
  40.9 52.1 %shard_map.186 = bf16[128,512]{1,0:T(8,128)(2,1)} custom-call(bf16[512,128]{1,0:T(8,128)(2,1)} %get-tuple-element.5.part_ref, s32[128,1]{1,0:T(8,128)} %copy.49.src_ref, f32[128,16]{1,0:T(8,128)} %fusion.index_ref, f32[128,16]{1,0:T(8,128)} %broadcast_subtract_fusion.gap_ref, f32[1,128]{1,0:T(1,128)} %bitcast.19, f32[1,128]{1,0:T(1,128)} %bitcast.21, ...), custom_call_target="tpu_custom_call" | custom-call | tf_op jit(solution)/shard_map/pallas_call | solution.py:265
  93.1 0.0 copy-done
  93.1 0.7 copy.53
  93.8 1.6 %copy.54 = bf16[128,512]{1,0:T(8,128)(2,1)} copy(bf16[128,512]{1,0:T(8,128)(2,1)} %shard_map.186) | data formatting | bytes 262144
  (2 shorter events, 0.0 us)
Async XLA Ops:
  4.9 33.6 %copy-start.3 = (s32[128,16]{0,1:T(8,128)S(1)}, s32[128,16]{0,1:T(8,128)}, u32[]{:S(2)}) copy-start(s32[128,16]{0,1:T(8,128)} %param.26) | copy-start | bytes 24580
  4.9 34.4 %copy-start.1 = (s32[128,16,1]{0,2,1:T(1,128)S(1)}, s32[128,16,1]{0,2,1:T(1,128)}, u32[]{:S(2)}) copy-start(s32[128,16,1]{0,2,1:T(1,128)} %param.24) | copy-start | bytes 24580
  4.9 34.5 %copy-start.2 = (s32[128,16]{0,1:T(8,128)S(1)}, s32[128,16]{0,1:T(8,128)}, u32[]{:S(2)}) copy-start(s32[128,16]{0,1:T(8,128)} %param.25) | copy-start | bytes 24580
  4.9 35.3 %copy-start.4 = (s32[128]{0:T(128)S(1)}, s32[128]{0:T(128)}, u32[]{:S(2)}) copy-start(s32[128]{0:T(128)} %param.20) | copy-start | bytes 1540
  40.2 52.9 %copy-start = (f32[512,128]{1,0:T(8,128)S(1)}, f32[512,128]{1,0:T(8,128)}, u32[]{:S(2)}) copy-start(f32[512,128]{1,0:T(8,128)} %get-tuple-element.12) | copy-start | bytes 786436
